TPU v7x, 32 devices: a whole 2x2x4 slice. The times are simulated.
32 devices in a mesh: lead: 4 (over x, core), space: 8 (over z, y).
Axes of the slice: x: 2, y: 2, z: 4, core: 2. Of those that a mesh axis runs over, the one named last changes fastest.
Arguments:
- states: bfloat16 [4, 4, 64, 128, 768], P('lead', None, 'space'), may hold values from -6 to 6
- filter_in: bfloat16 [2, 8, 96, 96], replicated, may hold values from -0.4375 to 0.4375
- filter_out: bfloat16 [2, 8, 96, 96], replicated, may hold values from -0.21875 to 0.21875
- filter_bias: float32 [2, 768], replicated, may hold values from -6 to 6
- decoder: bfloat16 [768, 128], replicated, may hold values from -0.5 to 0.5
- obs_value: float32 [4, 4, 32768], P('lead', None, 'space'), may hold values from -6 to 6
- obs_weight: float32 [4, 32768], P('lead', 'space'), may hold values from 0.5 to 2
- obs_index: int32 [4, 32768], P('lead', 'space'), may hold values from 0 to 131071
- block_dest: int32 [4, 256], P('lead', 'space'), may hold values from 0 to 7, as said below
- block_count: int32 [4, 256], P('lead', 'space'), may hold values from 96 to 128
Outputs:
- adjoint_fields: bfloat16 [4, 4, 64, 128, 768], P('lead', None, 'space')
Inputs may be any that keep to these rules, and one draw needn't show every extreme that they name: `block_dest`: at most 8 blocks of one owner in one section name the same tile, and in each section one tile is named by exactly 8 blocks of every owner.
All inputs are finite; a program needn't handle non-finite values.
Results may differ from a plain program's by a relative error of at most 0.017.
Values may be sent and summed in bfloat16 or wider, within the bound.
A program may use at most 192 MiB of HBM per device.

v0:
```python
import math

import jax
import jax.numpy as jnp
from jax import lax
from jax.sharding import PartitionSpec as P

OBS_BLK = 128


root_scale = math.sqrt(2.0 / math.pi)
cubic_term = 0.044715


def gelu_slope(values):
    argument = root_scale * (values + cubic_term * values * values * values)
    tangent = jnp.tanh(argument)
    return 0.5 * (1.0 + tangent) + 0.5 * values * (1.0 - tangent * tangent) * root_scale * (
        1.0 + 3.0 * cubic_term * values * values
    )


def wave_table(row_count, col_count, length):
    row_index = lax.broadcasted_iota(jnp.int32, (row_count, col_count), 0)
    col_index = lax.broadcasted_iota(jnp.int32, (row_count, col_count), 1)
    angles = (row_index * col_index % length).astype(jnp.float32) * (2.0 * math.pi / length)
    return (jnp.cos(angles), jnp.sin(angles))


def make_tables(lon_len, lat_len):
    mode_count = lon_len // 2
    lon_scale = 1.0 / math.sqrt(lon_len)
    lat_scale = 1.0 / math.sqrt(lat_len)
    cos_fore, sin_fore = wave_table(lon_len, mode_count, lon_len)
    cos_back, sin_back = wave_table(mode_count, lon_len, lon_len)
    factor = jnp.where(lax.broadcasted_iota(jnp.int32, (mode_count, 1), 0) == 0, 1.0, 2.0).astype(
        jnp.float32
    )
    cos_lat, sin_lat = wave_table(lat_len, lat_len, lat_len)
    lon_cos = (cos_fore * lon_scale).astype(jnp.bfloat16)
    lon_sin = (-sin_fore * lon_scale).astype(jnp.bfloat16)
    back_cos = (factor * cos_back * lon_scale).astype(jnp.bfloat16)
    back_sin = (-factor * sin_back * lon_scale).astype(jnp.bfloat16)
    lat_cos = (cos_lat * lat_scale).astype(jnp.bfloat16)
    lat_sin = (sin_lat * lat_scale).astype(jnp.bfloat16)
    return (lon_cos, lon_sin, back_cos, back_sin, lat_cos, lat_sin)


def contract(pattern, left_op, right_op):
    return jnp.einsum(pattern, left_op, right_op, preferred_element_type=jnp.float32)


def block_mix(operand, matrix):
    split_view = operand.reshape(operand.shape[:-1] + (matrix.shape[0], matrix.shape[1]))
    return contract("...ni,nio->...no", split_view, matrix).reshape(operand.shape)


def block_mix_t(operand, matrix):
    split_view = operand.reshape(operand.shape[:-1] + (matrix.shape[0], matrix.shape[2]))
    return contract("...no,nio->...ni", split_view, matrix).reshape(operand.shape)


def shards(
    states,
    filter_in,
    filter_out,
    filter_bias,
    decoder,
    obs_value,
    obs_weight,
    obs_index,
    block_dest,
    block_count,
):
    fields = states[0]
    member_count, lat_local, lon_len, channels = fields.shape
    tiles = lax.axis_size("space")
    lon_cos, lon_sin, back_cos, back_sin, lat_cos, lat_sin = make_tables(lon_len, lat_local * tiles)
    spec_re = contract("mfnc,nk->mfkc", fields, lon_cos).astype(jnp.bfloat16)
    spec_im = contract("mfnc,nk->mfkc", fields, lon_sin).astype(jnp.bfloat16)
    piece_re = lax.all_to_all(spec_re, "space", split_axis=2, concat_axis=1, tiled=True)
    piece_im = lax.all_to_all(spec_im, "space", split_axis=2, concat_axis=1, tiled=True)
    mode_re = (
        contract("pf,mfkc->mpkc", lat_cos, piece_re) + contract("pf,mfkc->mpkc", lat_sin, piece_im)
    ).astype(jnp.bfloat16)
    mode_im = (
        contract("pf,mfkc->mpkc", lat_cos, piece_im) - contract("pf,mfkc->mpkc", lat_sin, piece_re)
    ).astype(jnp.bfloat16)
    pre_re = block_mix(mode_re, filter_in[0]) - block_mix(mode_im, filter_in[1]) + filter_bias[0]
    pre_im = block_mix(mode_re, filter_in[1]) + block_mix(mode_im, filter_in[0]) + filter_bias[1]
    slope_re = gelu_slope(pre_re)
    slope_im = gelu_slope(pre_im)
    block_total = block_dest.shape[1]
    slot_cap = 2 * ((block_total + tiles - 1) // tiles)
    live_rows = lax.broadcasted_iota(jnp.int32, (block_total, OBS_BLK), 1) < block_count[0][:, None]
    weight_rows = jnp.where(live_rows, obs_weight[0].reshape(block_total, OBS_BLK), 0.0)
    index_rows = obs_index[0].reshape(block_total, OBS_BLK).astype(jnp.float32)
    value_rows = jnp.swapaxes(obs_value[0].reshape(member_count, block_total, OBS_BLK), 0, 1)
    payload = jnp.concatenate([weight_rows[:, None], index_rows[:, None], value_rows], axis=1)
    targets = block_dest[0]
    matches = (targets[:, None] == lax.broadcasted_iota(jnp.int32, (block_total, tiles), 1)).astype(
        jnp.int32
    )
    earlier = jnp.cumsum(matches, axis=0) - matches
    slot_rank = jnp.sum(earlier * matches, axis=1)
    positions = targets * slot_cap + slot_rank
    outbox = (
        jnp.zeros((tiles * slot_cap, member_count + 2, OBS_BLK), jnp.float32)
        .at[positions]
        .set(payload)
    )
    received = lax.all_to_all(outbox, "space", split_axis=0, concat_axis=0, tiled=True)
    got_weight = received[:, 0].reshape(-1)
    got_index = received[:, 1].reshape(-1).astype(jnp.int32)
    got_value = jnp.swapaxes(received[:, 2:], 0, 1).reshape(member_count, -1)
    levels = decoder.shape[1]
    decoded = contract("mfnc,cv->mfnv", fields, decoder).reshape(member_count, -1)
    innovation = got_weight[None, :] * (decoded[:, got_index] - got_value)
    spread_sum = jnp.zeros_like(decoded).at[:, got_index].add(innovation).astype(jnp.bfloat16)
    forcing = contract(
        "mfnv,cv->mfnc", spread_sum.reshape(member_count, lat_local, lon_len, levels), decoder
    )

    def adjoint_layer(incoming, gain_re, gain_im):
        back_re = contract("mfnc,kn->mfkc", incoming, back_cos).astype(jnp.bfloat16)
        back_im = contract("mfnc,kn->mfkc", incoming, back_sin).astype(jnp.bfloat16)
        wave_re, wave_im = (
            lax.all_to_all(back_re, "space", split_axis=2, concat_axis=1, tiled=True),
            lax.all_to_all(back_im, "space", split_axis=2, concat_axis=1, tiled=True),
        )
        out_re = (
            contract("fp,mfkc->mpkc", lat_cos, wave_re)
            + contract("fp,mfkc->mpkc", lat_sin, wave_im)
        ).astype(jnp.bfloat16)
        out_im = (
            contract("fp,mfkc->mpkc", lat_cos, wave_im)
            - contract("fp,mfkc->mpkc", lat_sin, wave_re)
        ).astype(jnp.bfloat16)
        hid_re = block_mix_t(out_re, filter_out[0]) + block_mix_t(out_im, filter_out[1])
        hid_im = block_mix_t(out_im, filter_out[0]) - block_mix_t(out_re, filter_out[1])
        act_re = (hid_re * gain_re).astype(jnp.bfloat16)
        act_im = (hid_im * gain_im).astype(jnp.bfloat16)
        grad_re = (block_mix_t(act_re, filter_in[0]) + block_mix_t(act_im, filter_in[1])).astype(
            jnp.bfloat16
        )
        grad_im = (block_mix_t(act_im, filter_in[0]) - block_mix_t(act_re, filter_in[1])).astype(
            jnp.bfloat16
        )
        lat_re = (
            contract("pf,mpkc->mfkc", lat_cos, grad_re)
            - contract("pf,mpkc->mfkc", lat_sin, grad_im)
        ).astype(jnp.bfloat16)
        lat_im = (
            contract("pf,mpkc->mfkc", lat_sin, grad_re)
            + contract("pf,mpkc->mfkc", lat_cos, grad_im)
        ).astype(jnp.bfloat16)
        ret_re, ret_im = (
            lax.all_to_all(lat_re, "space", split_axis=1, concat_axis=2, tiled=True),
            lax.all_to_all(lat_im, "space", split_axis=1, concat_axis=2, tiled=True),
        )
        return contract("mfkc,nk->mfnc", ret_re, lon_cos) + contract(
            "mfkc,nk->mfnc", ret_im, lon_sin
        )

    lead_count = lax.axis_size("lead")
    moved_forcing, moved_re, moved_im = (
        lax.all_to_all(
            forcing[None].astype(jnp.bfloat16), "lead", split_axis=1, concat_axis=0, tiled=True
        ).astype(jnp.float32),
        lax.all_to_all(
            slope_re[None].astype(jnp.bfloat16), "lead", split_axis=1, concat_axis=0, tiled=True
        ).astype(jnp.float32),
        lax.all_to_all(
            slope_im[None].astype(jnp.bfloat16), "lead", split_axis=1, concat_axis=0, tiled=True
        ).astype(jnp.float32),
    )
    share = member_count // lead_count

    def local_turn(counter, state_pair):
        incoming, result = state_pair
        section = lead_count - 1 - counter
        sec_re = lax.dynamic_index_in_dim(moved_re, section, 0, keepdims=False)
        sec_im = lax.dynamic_index_in_dim(moved_im, section, 0, keepdims=False)
        sec_forcing = lax.dynamic_index_in_dim(moved_forcing, section, 0, keepdims=False)
        updated = (
            incoming.astype(jnp.float32) + adjoint_layer(incoming, sec_re, sec_im) + sec_forcing
        ).astype(jnp.bfloat16)
        return (updated, lax.dynamic_update_index_in_dim(result, updated, section, 0))

    start_field = jnp.zeros((share,) + fields.shape[1:], jnp.bfloat16)
    start_result = jnp.zeros((lead_count, share) + fields.shape[1:], jnp.bfloat16)
    grouped = lax.fori_loop(0, lead_count, local_turn, (start_field, start_result))[1]
    return lax.all_to_all(grouped, "lead", split_axis=0, concat_axis=1, tiled=True)


def solution(mesh):
    placed = (
        P("lead", None, "space", None, None),
        P(),
        P(),
        P(),
        P(),
        P("lead", None, "space"),
        P("lead", "space"),
        P("lead", "space"),
        P("lead", "space"),
        P("lead", "space"),
    )
    return jax.shard_map(
        shards,
        mesh=mesh,
        in_specs=placed,
        out_specs=P("lead", None, "space", None, None),
        check_vma=False,
    )
```

profile of v0, /device:TPU:0, one launch (start us, length us, event | category | flops | bytes accessed | tf_op | source)
XLA Modules:
  0.0 1421.2 jit_solution(11141297752720320979)
XLA Ops:
  37.6 62.8 %all-to-all-done.4 = bf16[4,8,64,768]{3,1,0,2:T(8,128)(2,1)S(1)} async-done(((bf16[4,8,64,768]{3,1,0,2:T(8,128)(2,1)}), bf16[4,8,64,768]{3,1,0,2:T(8,128)(2,1)S(1)}, u32[]{:S(2)}, u32[]{:S(2)}) %all-to-all-start.4) | async-done | bytes 3145760 | tf_op jit(solution)/shard_map/all_to_all | solution.py:81
  111.0 33.7 %copy.209 = f32[4,8,128,128]{0,3,2,1:T(8,128)} copy(f32[4,8,128,128]{3,2,1,0:T(8,128)} %fusion.206) | data formatting | bytes 4194304 | tf_op jit(solution)/shard_map/reshape | solution.py:117
  145.7 119.2 %gather_fusion = f32[8192,4]{1,0:T(8,128)} fusion(f32[4,131072]{0,1:T(8,128)} %bitcast.57, s32[8192]{0:T(1024)S(1)} %broadcast_clamp_fusion.1), kind=kCustom, calls=%fused_computation | custom fusion | bytes 294912 | tf_op jit(solution)/shard_map/gather | solution.py:118
  279.0 123.1 %scatter_custom_fusion.1 = f32[4,131072]{0,1:T(8,128)} fusion(s32[8192]{0:T(1024)S(1)} %get-tuple-element.490, f32[]{:T(128)} %constant.130.clone.1, f32[8192,4]{1,0:T(8,128)} %copy.189, s32[8192]{0:T(1024)S(1)} %broadcast_clamp_fusion), kind=kCustom, calls=%fused_computation.194 | custom fusion | flops 32768 | bytes 2097664 | tf_op jit(solution)/shard_map/scatter-add | solution.py:119
  402.0 32.7 %convert_element_type.425 = bf16[4,131072]{0,1:T(8,128)(2,1)} convert(f32[4,131072]{0,1:T(8,128)} %scatter_custom_fusion.1) | non-fusion elementwise | flops 524288 | bytes 3145728 | tf_op jit(solution)/shard_map/convert_element_type | solution.py:119
  434.7 28.4 %copy.190 = bf16[4,8,128,128]{3,2,1,0:T(8,128)(2,1)} copy(bf16[4,8,128,128]{0,3,2,1:T(8,128)(2,1)} %bitcast.483) | data formatting | bytes 2097152 | tf_op jit(solution)/shard_map/reshape | solution.py:121
  468.7 161.7 %all-to-all-start.9 = ((bf16[1,4,8,128,768]{4,3,2,0,1:T(8,128)(2,1)}), bf16[1,4,8,128,768]{4,3,2,0,1:T(8,128)(2,1)}, u32[]{:S(2)}, u32[]{:S(2)}) async-start(bf16[1,4,8,128,768]{4,3,2,0,1:T(8,128)(2,1)} %convert_bitcast_fusion), calls=%async_computation.9 | async-start | bytes 12582912 | tf_op jit(solution)/shard_map/all_to_all | solution.py:167
  688.5 12.7 all-to-all-done.9
  761.9 23.1 %all-to-all-done.6 = bf16[1,4,64,8,768]{4,3,2,0,1:T(8,128)(2,1)} async-done(((bf16[1,4,64,8,768]{4,3,2,0,1:T(8,128)(2,1)}), bf16[1,4,64,8,768]{4,3,2,0,1:T(8,128)(2,1)}, u32[]{:S(2)}, u32[]{:S(2)}) %all-to-all-start.6) | async-done | bytes 3145760 | tf_op jit(solution)/shard_map/all_to_all | solution.py:170
  793.4 550.2 %while.19 = (s32[]{:T(128)}, bf16[1,8,128,768]{2,3,1,0:T(8,128)(2,1)S(1)}, bf16[4,1,8,128,768]{4,3,2,1,0:T(8,128)(2,1)}, bf16[2,8,96,96]{3,2,1,0:T(8,128)(2,1)},...) while((s32[]{:T(128)}, ...), condition=%wide.region_5.6_spmd.clone.clone, body=%wide.region_4.5_spmd.clone.clone.sunk | while | flops 1424515072 | bytes 177079392 | solution.py:192
  795.8 18.9 %all-to-all-start.1 = ((bf16[1,8,64,768]{3,1,0,2:T(8,128)(2,1)}), bf16[1,8,64,768]{3,1,0,2:T(8,128)(2,1)S(1)}, u32[]{:S(2)}, u32[]{:S(2)}) async-start(bf16[1,8,64,768]{3,1,0,2:T(8,128)(2,1)} %copy.321), calls=%async_computation.1 | async-start | bytes 1572864 | tf_op jit(solution)/shard_map/while/body/eval_jaxpr/all_to_all | solution.py:129
  816.8 18.0 %all-to-all-done.1 = bf16[1,8,64,768]{3,1,0,2:T(8,128)(2,1)S(1)} async-done(((bf16[1,8,64,768]{3,1,0,2:T(8,128)(2,1)}), bf16[1,8,64,768]{3,1,0,2:T(8,128)(2,1)S(1)}, u32[]{:S(2)}, u32[]{:S(2)}) %all-to-all-start.1) | async-done | bytes 786464 | tf_op jit(solution)/shard_map/while/body/eval_jaxpr/all_to_all | solution.py:129
  892.4 18.1 %all-to-all-done.2 = bf16[1,64,8,768]{3,2,0,1:T(8,128)(2,1)S(1)} async-done(((bf16[1,64,8,768]{3,2,0,1:T(8,128)(2,1)}), bf16[1,64,8,768]{3,2,0,1:T(8,128)(2,1)S(1)}, u32[]{:S(2)}, u32[]{:S(2)}) %all-to-all-start.2) | async-done | bytes 786464 | tf_op jit(solution)/shard_map/while/body/eval_jaxpr/all_to_all | solution.py:158
  923.1 11.5 all-to-all-done.3
  951.3 16.8 %all-to-all-done.1 = bf16[1,8,64,768]{3,1,0,2:T(8,128)(2,1)S(1)} async-done(((bf16[1,8,64,768]{3,1,0,2:T(8,128)(2,1)}), bf16[1,8,64,768]{3,1,0,2:T(8,128)(2,1)S(1)}, u32[]{:S(2)}, u32[]{:S(2)}) %all-to-all-start.1) | async-done | bytes 786464 | tf_op jit(solution)/shard_map/while/body/eval_jaxpr/all_to_all | solution.py:129
  1025.8 18.1 %all-to-all-done.2 = bf16[1,64,8,768]{3,2,0,1:T(8,128)(2,1)S(1)} async-done(((bf16[1,64,8,768]{3,2,0,1:T(8,128)(2,1)}), bf16[1,64,8,768]{3,2,0,1:T(8,128)(2,1)S(1)}, u32[]{:S(2)}, u32[]{:S(2)}) %all-to-all-start.2) | async-done | bytes 786464 | tf_op jit(solution)/shard_map/while/body/eval_jaxpr/all_to_all | solution.py:158
  1056.5 11.5 all-to-all-done.3
  1085.2 16.8 %all-to-all-done.1 = bf16[1,8,64,768]{3,1,0,2:T(8,128)(2,1)S(1)} async-done(((bf16[1,8,64,768]{3,1,0,2:T(8,128)(2,1)}), bf16[1,8,64,768]{3,1,0,2:T(8,128)(2,1)S(1)}, u32[]{:S(2)}, u32[]{:S(2)}) %all-to-all-start.1) | async-done | bytes 786464 | tf_op jit(solution)/shard_map/while/body/eval_jaxpr/all_to_all | solution.py:129
  1159.7 18.1 %all-to-all-done.2 = bf16[1,64,8,768]{3,2,0,1:T(8,128)(2,1)S(1)} async-done(((bf16[1,64,8,768]{3,2,0,1:T(8,128)(2,1)}), bf16[1,64,8,768]{3,2,0,1:T(8,128)(2,1)S(1)}, u32[]{:S(2)}, u32[]{:S(2)}) %all-to-all-start.2) | async-done | bytes 786464 | tf_op jit(solution)/shard_map/while/body/eval_jaxpr/all_to_all | solution.py:158
  1190.4 11.5 all-to-all-done.3
  1219.0 16.8 %all-to-all-done.1 = bf16[1,8,64,768]{3,1,0,2:T(8,128)(2,1)S(1)} async-done(((bf16[1,8,64,768]{3,1,0,2:T(8,128)(2,1)}), bf16[1,8,64,768]{3,1,0,2:T(8,128)(2,1)S(1)}, u32[]{:S(2)}, u32[]{:S(2)}) %all-to-all-start.1) | async-done | bytes 786464 | tf_op jit(solution)/shard_map/while/body/eval_jaxpr/all_to_all | solution.py:129
  1293.6 18.1 %all-to-all-done.2 = bf16[1,64,8,768]{3,2,0,1:T(8,128)(2,1)S(1)} async-done(((bf16[1,64,8,768]{3,2,0,1:T(8,128)(2,1)}), bf16[1,64,8,768]{3,2,0,1:T(8,128)(2,1)S(1)}, u32[]{:S(2)}, u32[]{:S(2)}) %all-to-all-start.2) | async-done | bytes 786464 | tf_op jit(solution)/shard_map/while/body/eval_jaxpr/all_to_all | solution.py:158
  1324.2 11.5 all-to-all-done.3
  1343.7 74.6 %all_to_all.252 = bf16[4,1,8,128,768]{4,3,2,1,0:T(8,128)(2,1)S(1)} all-to-all(bf16[4,1,8,128,768]{4,3,2,1,0:T(8,128)(2,1)} %get-tuple-element.353), channel_id=1, replica_groups=mesh['lead'=4,'space'=8] {'lead'}, dimensions={0} | all-to-all | bytes 12582912 | tf_op jit(solution)/shard_map/all_to_all | solution.py:193
  (310 shorter events, 542.4 us)
Async XLA Ops:
  9.0 16.2 %all-to-all-start.8 = ((f32[64,6,128]{2,1,0:T(8,128)}), f32[64,6,128]{2,1,0:T(8,128)S(1)}, u32[]{:S(2)}, u32[]{:S(2)}) async-start(f32[64,6,128]{2,1,0:T(8,128)} %scatter_fusion), calls=%async_computation.8 | async-start | bytes 524288 | tf_op jit(solution)/shard_map/all_to_all | solution.py:112
  25.9 74.5 %all-to-all-start.4 = ((bf16[4,8,64,768]{3,1,0,2:T(8,128)(2,1)}), bf16[4,8,64,768]{3,1,0,2:T(8,128)(2,1)S(1)}, u32[]{:S(2)}, u32[]{:S(2)}) async-start(bf16[4,8,64,768]{3,1,0,2:T(8,128)(2,1)} %copy.172), calls=%async_computation.4 | async-start | bytes 6291456 | tf_op jit(solution)/shard_map/all_to_all | solution.py:81
  100.4 368.3 %all-to-all-start.5 = ((bf16[4,8,64,768]{3,1,0,2:T(8,128)(2,1)}), bf16[4,8,64,768]{3,1,0,2:T(8,128)(2,1)}, u32[]{:S(2)}, u32[]{:S(2)}) async-start(bf16[4,8,64,768]{3,1,0,2:T(8,128)(2,1)} %copy.174), calls=%async_computation.5 | async-start | bytes 6291456 | tf_op jit(solution)/shard_map/all_to_all | solution.py:82
  144.6 123.2 %slice-start = ((f32[64,6,128]{2,1,0:T(8,128)}), f32[64,1,128]{2,1,0:T(1,128)S(1)}, s32[]{:S(2)}) async-start(f32[64,6,128]{2,1,0:T(8,128)} %copy-done.14), calls=%async_computation.11 | async-start | bytes 65536 | tf_op jit(solution)/shard_map/slice | solution.py:113
  468.7 161.7 %copy-start.15 = (f32[2,768]{1,0:T(2,128)S(1)}, f32[2,768]{1,0:T(2,128)}, u32[]{:S(2)}) copy-start(f32[2,768]{1,0:T(2,128)} %param.15) | copy-start | bytes 18436
  468.7 232.5 %all-to-all-start.9 = ((bf16[1,4,8,128,768]{4,3,2,0,1:T(8,128)(2,1)}), bf16[1,4,8,128,768]{4,3,2,0,1:T(8,128)(2,1)}, u32[]{:S(2)}, u32[]{:S(2)}) async-start(bf16[1,4,8,128,768]{4,3,2,0,1:T(8,128)(2,1)} %convert_bitcast_fusion), calls=%async_computation.9 | async-start | bytes 12582912 | tf_op jit(solution)/shard_map/all_to_all | solution.py:167
  701.2 42.0 %all-to-all-start.7 = ((bf16[1,4,64,8,768]{4,3,2,0,1:T(8,128)(2,1)}), bf16[1,4,64,8,768]{4,3,2,0,1:T(8,128)(2,1)}, u32[]{:S(2)}, u32[]{:S(2)}) async-start(bf16[1,4,64,8,768]{4,3,2,0,1:T(8,128)(2,1)} %fusion.237), calls=%async_computation.7 | async-start | bytes 6291456 | tf_op jit(solution)/shard_map/all_to_all | solution.py:173
  743.2 41.7 %all-to-all-start.6 = ((bf16[1,4,64,8,768]{4,3,2,0,1:T(8,128)(2,1)}), bf16[1,4,64,8,768]{4,3,2,0,1:T(8,128)(2,1)}, u32[]{:S(2)}, u32[]{:S(2)}) async-start(bf16[1,4,64,8,768]{4,3,2,0,1:T(8,128)(2,1)} %fusion.238), calls=%async_computation.6 | async-start | bytes 6291456 | tf_op jit(solution)/shard_map/all_to_all | solution.py:170
  795.8 38.9 %all-to-all-start.1 = ((bf16[1,8,64,768]{3,1,0,2:T(8,128)(2,1)}), bf16[1,8,64,768]{3,1,0,2:T(8,128)(2,1)S(1)}, u32[]{:S(2)}, u32[]{:S(2)}) async-start(bf16[1,8,64,768]{3,1,0,2:T(8,128)(2,1)} %copy.321), calls=%async_computation.1 | async-start | bytes 1572864 | tf_op jit(solution)/shard_map/while/body/eval_jaxpr/all_to_all | solution.py:129
  834.7 23.9 %all-to-all-start = ((bf16[1,8,64,768]{3,1,0,2:T(8,128)(2,1)}), bf16[1,8,64,768]{3,1,0,2:T(8,128)(2,1)S(1)}, u32[]{:S(2)}, u32[]{:S(2)}) async-start(bf16[1,8,64,768]{3,1,0,2:T(8,128)(2,1)} %copy.320), calls=%async_computation | async-start | bytes 1572864 | tf_op jit(solution)/shard_map/while/body/eval_jaxpr/all_to_all | solution.py:128
  886.5 23.9 %all-to-all-start.2 = ((bf16[1,64,8,768]{3,2,0,1:T(8,128)(2,1)}), bf16[1,64,8,768]{3,2,0,1:T(8,128)(2,1)S(1)}, u32[]{:S(2)}, u32[]{:S(2)}) async-start(bf16[1,64,8,768]{3,2,0,1:T(8,128)(2,1)} %copy.324), calls=%async_computation.2 | async-start | bytes 1572864 | tf_op jit(solution)/shard_map/while/body/eval_jaxpr/all_to_all | solution.py:158
  910.5 24.1 %all-to-all-start.3 = ((bf16[1,64,8,768]{3,2,0,1:T(8,128)(2,1)}), bf16[1,64,8,768]{3,2,0,1:T(8,128)(2,1)}, u32[]{:S(2)}, u32[]{:S(2)}) async-start(bf16[1,64,8,768]{3,2,0,1:T(8,128)(2,1)} %copy.325), calls=%async_computation.3 | async-start | bytes 1572864 | tf_op jit(solution)/shard_map/while/body/eval_jaxpr/all_to_all | solution.py:159
  944.2 23.9 %all-to-all-start.1 = ((bf16[1,8,64,768]{3,1,0,2:T(8,128)(2,1)}), bf16[1,8,64,768]{3,1,0,2:T(8,128)(2,1)S(1)}, u32[]{:S(2)}, u32[]{:S(2)}) async-start(bf16[1,8,64,768]{3,1,0,2:T(8,128)(2,1)} %copy.321), calls=%async_computation.1 | async-start | bytes 1572864 | tf_op jit(solution)/shard_map/while/body/eval_jaxpr/all_to_all | solution.py:129
  968.1 23.9 %all-to-all-start = ((bf16[1,8,64,768]{3,1,0,2:T(8,128)(2,1)}), bf16[1,8,64,768]{3,1,0,2:T(8,128)(2,1)S(1)}, u32[]{:S(2)}, u32[]{:S(2)}) async-start(bf16[1,8,64,768]{3,1,0,2:T(8,128)(2,1)} %copy.320), calls=%async_computation | async-start | bytes 1572864 | tf_op jit(solution)/shard_map/while/body/eval_jaxpr/all_to_all | solution.py:128
  1019.9 23.9 %all-to-all-start.2 = ((bf16[1,64,8,768]{3,2,0,1:T(8,128)(2,1)}), bf16[1,64,8,768]{3,2,0,1:T(8,128)(2,1)S(1)}, u32[]{:S(2)}, u32[]{:S(2)}) async-start(bf16[1,64,8,768]{3,2,0,1:T(8,128)(2,1)} %copy.324), calls=%async_computation.2 | async-start | bytes 1572864 | tf_op jit(solution)/shard_map/while/body/eval_jaxpr/all_to_all | solution.py:158
  1043.9 24.1 %all-to-all-start.3 = ((bf16[1,64,8,768]{3,2,0,1:T(8,128)(2,1)}), bf16[1,64,8,768]{3,2,0,1:T(8,128)(2,1)}, u32[]{:S(2)}, u32[]{:S(2)}) async-start(bf16[1,64,8,768]{3,2,0,1:T(8,128)(2,1)} %copy.325), calls=%async_computation.3 | async-start | bytes 1572864 | tf_op jit(solution)/shard_map/while/body/eval_jaxpr/all_to_all | solution.py:159
  1078.1 23.9 %all-to-all-start.1 = ((bf16[1,8,64,768]{3,1,0,2:T(8,128)(2,1)}), bf16[1,8,64,768]{3,1,0,2:T(8,128)(2,1)S(1)}, u32[]{:S(2)}, u32[]{:S(2)}) async-start(bf16[1,8,64,768]{3,1,0,2:T(8,128)(2,1)} %copy.321), calls=%async_computation.1 | async-start | bytes 1572864 | tf_op jit(solution)/shard_map/while/body/eval_jaxpr/all_to_all | solution.py:129
  1102.0 23.9 %all-to-all-start = ((bf16[1,8,64,768]{3,1,0,2:T(8,128)(2,1)}), bf16[1,8,64,768]{3,1,0,2:T(8,128)(2,1)S(1)}, u32[]{:S(2)}, u32[]{:S(2)}) async-start(bf16[1,8,64,768]{3,1,0,2:T(8,128)(2,1)} %copy.320), calls=%async_computation | async-start | bytes 1572864 | tf_op jit(solution)/shard_map/while/body/eval_jaxpr/all_to_all | solution.py:128
  1153.8 23.9 %all-to-all-start.2 = ((bf16[1,64,8,768]{3,2,0,1:T(8,128)(2,1)}), bf16[1,64,8,768]{3,2,0,1:T(8,128)(2,1)S(1)}, u32[]{:S(2)}, u32[]{:S(2)}) async-start(bf16[1,64,8,768]{3,2,0,1:T(8,128)(2,1)} %copy.324), calls=%async_computation.2 | async-start | bytes 1572864 | tf_op jit(solution)/shard_map/while/body/eval_jaxpr/all_to_all | solution.py:158
  1177.7 24.1 %all-to-all-start.3 = ((bf16[1,64,8,768]{3,2,0,1:T(8,128)(2,1)}), bf16[1,64,8,768]{3,2,0,1:T(8,128)(2,1)}, u32[]{:S(2)}, u32[]{:S(2)}) async-start(bf16[1,64,8,768]{3,2,0,1:T(8,128)(2,1)} %copy.325), calls=%async_computation.3 | async-start | bytes 1572864 | tf_op jit(solution)/shard_map/while/body/eval_jaxpr/all_to_all | solution.py:159
  1212.0 23.9 %all-to-all-start.1 = ((bf16[1,8,64,768]{3,1,0,2:T(8,128)(2,1)}), bf16[1,8,64,768]{3,1,0,2:T(8,128)(2,1)S(1)}, u32[]{:S(2)}, u32[]{:S(2)}) async-start(bf16[1,8,64,768]{3,1,0,2:T(8,128)(2,1)} %copy.321), calls=%async_computation.1 | async-start | bytes 1572864 | tf_op jit(solution)/shard_map/while/body/eval_jaxpr/all_to_all | solution.py:129
  1235.8 23.9 %all-to-all-start = ((bf16[1,8,64,768]{3,1,0,2:T(8,128)(2,1)}), bf16[1,8,64,768]{3,1,0,2:T(8,128)(2,1)S(1)}, u32[]{:S(2)}, u32[]{:S(2)}) async-start(bf16[1,8,64,768]{3,1,0,2:T(8,128)(2,1)} %copy.320), calls=%async_computation | async-start | bytes 1572864 | tf_op jit(solution)/shard_map/while/body/eval_jaxpr/all_to_all | solution.py:128
  1287.7 23.9 %all-to-all-start.2 = ((bf16[1,64,8,768]{3,2,0,1:T(8,128)(2,1)}), bf16[1,64,8,768]{3,2,0,1:T(8,128)(2,1)S(1)}, u32[]{:S(2)}, u32[]{:S(2)}) async-start(bf16[1,64,8,768]{3,2,0,1:T(8,128)(2,1)} %copy.324), calls=%async_computation.2 | async-start | bytes 1572864 | tf_op jit(solution)/shard_map/while/body/eval_jaxpr/all_to_all | solution.py:158
  1311.6 24.1 %all-to-all-start.3 = ((bf16[1,64,8,768]{3,2,0,1:T(8,128)(2,1)}), bf16[1,64,8,768]{3,2,0,1:T(8,128)(2,1)}, u32[]{:S(2)}, u32[]{:S(2)}) async-start(bf16[1,64,8,768]{3,2,0,1:T(8,128)(2,1)} %copy.325), calls=%async_computation.3 | async-start | bytes 1572864 | tf_op jit(solution)/shard_map/while/body/eval_jaxpr/all_to_all | solution.py:159
  (42 other events, 288.6 us)
where the time goes:
time: 1430 us; the launch traced here: 1420 us
  local copies, waits for them, and re-layouts  383 us (27%)
  waiting for transfers between devices  329 us (23%)
  starting transfers between devices  263 us (18%)
  other arithmetic  202 us (14%)
  matrix products  168 us (12%)
  blocking collectives  74.6 us (5%)
    dot_general x92, matrix products, contract(): jnp.einsum(pattern, left_op, right_op, preferred_element_type=jnp.float32)  168 us
    all_to_all x1, starting transfers between devices, shards(): lax.all_to_all(forcing[None].astype(jnp.bfloat16), 'lead', split_axis=1,...  162 us
    scatter-add x3, other arithmetic, shards(): jnp.zeros_like(decoded).at[:, got_index].add(innovation)  129 us
    gather x2, local copies, waits for them, and re-layouts, shards(): innovation = got_weight[None, :] * (decoded[:, got_index] - got_value)  122 us
    all_to_all x1, blocking collectives, shards(): lax.all_to_all(grouped, 'lead', split_axis=0, concat_axis=1, tiled=True)  74.6 us
    all_to_all x4, waiting for transfers between devices, adjoint_layer(): lax.all_to_all(lat_re, 'space', split_axis=1, concat_axis=2, tiled=True)  72.3 us
    all_to_all x4, waiting for transfers between devices, adjoint_layer(): lax.all_to_all(back_im, 'space', split_axis=2, concat_axis=1, tiled=True)  68.3 us
    all_to_all x1, waiting for transfers between devices, shards(): lax.all_to_all(spec_re, 'space', split_axis=2, concat_axis=1, tiled=True)  62.8 us
  transfers between devices with their start and end apart: 22, of which 21 were waited for; matrix products, arithmetic and copies ran while one was open for 41% of the time, Pallas kernels for 0%

commit v1 on v0

--- a/solution.py
+++ b/solution.py
@@ -3,6 +3,8 @@
 import jax
 import jax.numpy as jnp
 from jax import lax
+from jax.experimental import pallas as pl
+from jax.experimental.pallas import tpu as pltpu
 from jax.sharding import PartitionSpec as P
 
 OBS_BLK = 128
@@ -58,6 +60,251 @@
 def block_mix_t(operand, matrix):
     split_view = operand.reshape(operand.shape[:-1] + (matrix.shape[0], matrix.shape[2]))
     return contract("...no,nio->...ni", split_view, matrix).reshape(operand.shape)
+
+
+VMEM_BYTES = 56 * 1024 * 1024
+
+
+def matmul(left, right):
+    return jnp.dot(left, right, preferred_element_type=jnp.float32)
+
+
+def rounded(values):
+    return values.astype(jnp.bfloat16).astype(jnp.float32)
+
+
+def turned(values):
+    half = values.shape[1] // 2
+    lanes = lax.broadcasted_iota(jnp.int32, values.shape, 1)
+    rolled = pltpu.roll(values, half, 1)
+    return jnp.where(lanes < half, rolled, -rolled)
+
+
+def doubled(values):
+    return jnp.concatenate([values, turned(values)], axis=0).astype(jnp.bfloat16)
+
+
+def observe_kernel(cell_ref, level_ref, row_ref, high_ref, low_ref, out_ref, total):
+    step = pl.program_id(0)
+
+    @pl.when(step == 0)
+    def _():
+        total[...] = jnp.zeros_like(total)
+
+    members, lats, levels, lons = out_ref.shape
+    rows = cell_ref.shape[1]
+    hot = (
+        (lax.broadcasted_iota(jnp.int32, (lats * lons, rows), 0) == cell_ref[...])
+        .astype(jnp.float32)
+        .astype(jnp.bfloat16)
+    )
+    at_level = lax.broadcasted_iota(jnp.int32, (levels, rows), 0) == level_ref[...]
+    picked = matmul(high_ref[...], hot) + matmul(low_ref[...], hot)
+    weight = row_ref[0:1, :]
+    spread = []
+    for m in range(members):
+        own = jnp.where(at_level, picked[m * levels : (m + 1) * levels], 0.0)
+        innovation = weight * (jnp.sum(own, axis=0, keepdims=True) - row_ref[m + 1 : m + 2, :])
+        spread.append(jnp.where(at_level, innovation, 0.0))
+    spread = jnp.concatenate(spread, axis=0)
+    high = spread.astype(jnp.bfloat16)
+    low = (spread - high.astype(jnp.float32)).astype(jnp.bfloat16)
+    dims = (((1,), (1,)), ((), ()))
+    total[...] += lax.dot_general(
+        high, hot, dims, preferred_element_type=jnp.float32
+    ) + lax.dot_general(low, hot, dims, preferred_element_type=jnp.float32)
+
+    @pl.when(step == pl.num_programs(0) - 1)
+    def _():
+        for m in range(members):
+            for f in range(lats):
+                out_ref[m, f] = total[
+                    m * levels : (m + 1) * levels, f * lons : (f + 1) * lons
+                ].astype(jnp.bfloat16)
+
+
+def observe(received, fields, decoder):
+    members, lats, lons, channels = fields.shape
+    levels = decoder.shape[1]
+    decoded = contract("mfnc,cv->mvfn", fields, decoder).reshape(members * levels, lats * lons)
+    high = decoded.astype(jnp.bfloat16)
+    low = (decoded - high.astype(jnp.float32)).astype(jnp.bfloat16)
+    flat = jnp.swapaxes(received, 0, 1).reshape(members + 2, -1)
+    count = flat.shape[1]
+    index = flat[1:2].astype(jnp.int32)
+    rows = jnp.concatenate([flat[:1], flat[2:]], axis=0)
+    chunk = next(size for size in (512, 256, 128) if count % size == 0)
+    whole = lambda i: (0, 0)
+    piece = lambda i: (0, i)
+    return pl.pallas_call(
+        observe_kernel,
+        grid=(count // chunk,),
+        in_specs=[
+            pl.BlockSpec((1, chunk), piece),
+            pl.BlockSpec((1, chunk), piece),
+            pl.BlockSpec((members + 1, chunk), piece),
+            pl.BlockSpec(high.shape, whole),
+            pl.BlockSpec(low.shape, whole),
+        ],
+        out_specs=pl.BlockSpec((members, lats, levels, lons), lambda i: (0, 0, 0, 0)),
+        out_shape=jax.ShapeDtypeStruct((members, lats, levels, lons), jnp.bfloat16),
+        scratch_shapes=[pltpu.VMEM((members * levels, lats * lons), jnp.float32)],
+        compiler_params=pltpu.CompilerParams(vmem_limit_bytes=VMEM_BYTES),
+        cost_estimate=pl.CostEstimate(
+            flops=8 * count * members * levels * lats * lons,
+            bytes_accessed=8 * members * levels * lats * lons,
+            transcendentals=0,
+        ),
+        name="observe",
+    )(index // levels, index % levels, rows, high, low)
+
+
+def slope_kernel(spec_ref, lat_ref, mix_ref, bias_ref, out_ref, hold):
+    lats, width, waves = spec_ref.shape
+
+    @pl.loop(0, lats, unroll=4)
+    def _(f):
+        hold[pl.ds(pl.multiple_of(f * width, 8), width), :] = spec_ref[f].astype(jnp.float32)
+
+    @pl.loop(0, width, unroll=8)
+    def _(c):
+        place = pl.ds(c, lats, stride=width)
+        hold[place, :] = rounded(matmul(lat_ref[...], doubled(hold[place, :])))
+
+    @pl.loop(0, lats, unroll=4)
+    def _(p):
+        modes = hold[pl.ds(pl.multiple_of(p * width, 8), width), :]
+        before = matmul(mix_ref[...], doubled(modes)) + bias_ref[...]
+        out_ref[p] = gelu_slope(before).astype(jnp.bfloat16)
+
+
+def slopes(spec, lat_fore, mix, bias):
+    lats, width, waves = spec.shape
+    return pl.pallas_call(
+        slope_kernel,
+        out_shape=jax.ShapeDtypeStruct(spec.shape, jnp.bfloat16),
+        scratch_shapes=[pltpu.VMEM((lats * width, waves), jnp.float32)],
+        compiler_params=pltpu.CompilerParams(vmem_limit_bytes=VMEM_BYTES),
+        cost_estimate=pl.CostEstimate(
+            flops=4 * lats * width * waves * (lats + width),
+            bytes_accessed=4 * lats * width * waves,
+            transcendentals=lats * width * waves,
+        ),
+        name="slopes",
+    )(spec, lat_fore, mix, bias)
+
+
+def adjoint_kernel(
+    in_ref,
+    gain_ref,
+    level_ref,
+    decoder_ref,
+    outer_ref,
+    inner_ref,
+    back_ref,
+    fore_ref,
+    ret_ref,
+    lift_ref,
+    out_ref,
+    hold,
+    force,
+):
+    width, lats, lons = in_ref.shape
+
+    @pl.loop(0, lats, unroll=8)
+    def _(f):
+        force[pl.ds(f, width, stride=lats), :] = matmul(decoder_ref[...], level_ref[f])
+
+    @pl.loop(0, width, unroll=8)
+    def _(c):
+        back = rounded(matmul(in_ref[c], back_ref[...]))
+        hold[pl.ds(c, lats, stride=width), :] = rounded(matmul(fore_ref[...], doubled(back)))
+
+    @pl.loop(0, lats, unroll=8)
+    def _(p):
+        place = pl.ds(pl.multiple_of(p * width, 8), width)
+        hidden = matmul(outer_ref[...], doubled(hold[place, :]))
+        act = rounded(hidden * gain_ref[p].astype(jnp.float32))
+        hold[place, :] = rounded(matmul(inner_ref[...], doubled(act)))
+
+    @pl.loop(0, width, unroll=8)
+    def _(c):
+        grad = doubled(hold[pl.ds(c, lats, stride=width), :])
+        waves = matmul(ret_ref[...], grad).astype(jnp.bfloat16)
+        added = matmul(waves, lift_ref[...]) + force[pl.ds(pl.multiple_of(c * lats, 8), lats), :]
+        out_ref[c] = (in_ref[c].astype(jnp.float32) + added).astype(jnp.bfloat16)
+
+
+def adjoint_step(incoming, gain, level_forcing, *weights):
+    width, lats, lons = incoming.shape
+    waves = gain.shape[2]
+    return pl.pallas_call(
+        adjoint_kernel,
+        out_shape=jax.ShapeDtypeStruct(incoming.shape, jnp.bfloat16),
+        scratch_shapes=[
+            pltpu.VMEM((lats * width, waves), jnp.float32),
+            pltpu.VMEM((lats * width, lons), jnp.float32),
+        ],
+        compiler_params=pltpu.CompilerParams(vmem_limit_bytes=VMEM_BYTES),
+        cost_estimate=pl.CostEstimate(
+            flops=8 * lats * width * waves * (lats + width + lons),
+            bytes_accessed=10 * lats * width * waves,
+            transcendentals=0,
+        ),
+        name="adjoint",
+    )(incoming, gain, level_forcing, *weights)
+
+
+def channel_plan(fields, filter_in, filter_out, filter_bias, decoder, received):
+    member_count, lat_local, lon_len, channels = fields.shape
+    tiles = lax.axis_size("space")
+    sections = lax.axis_size("lead")
+    me = lax.axis_index("space")
+    width = filter_in.shape[2]
+    lon_cos, lon_sin, back_cos, back_sin, lat_cos, lat_sin = make_tables(lon_len, lat_local * tiles)
+    lon_fore = jnp.concatenate([lon_cos, lon_sin], axis=1)
+    lon_back = jnp.concatenate([back_cos, back_sin], axis=0).T
+    lat_fore = jnp.concatenate([lat_cos, lat_sin], axis=1)
+    lat_back = jnp.concatenate([lat_cos.T, lat_sin.T], axis=1)
+    lat_ret = jnp.concatenate([lat_cos.T, -lat_sin.T], axis=1)
+    first = lax.dynamic_index_in_dim(filter_in, me, 1, keepdims=False)
+    second = lax.dynamic_index_in_dim(filter_out, me, 1, keepdims=False)
+    mix = jnp.concatenate([first[0].T, -first[1].T], axis=1)
+    outer = jnp.concatenate([second[0], second[1]], axis=1)
+    inner = jnp.concatenate([first[0], first[1]], axis=1)
+    bias_own = lax.dynamic_slice_in_dim(filter_bias, me * width, width, 1)
+    bias = jnp.repeat(bias_own.T, lon_len // 2, axis=1, total_repeat_length=lon_len)
+    decoder_own = lax.dynamic_slice_in_dim(decoder, me * width, width, 0)
+
+    gains = []
+    for m in range(member_count):
+        spec = contract("fnc,nk->fck", fields[m], lon_fore).astype(jnp.bfloat16)
+        spec = lax.all_to_all(spec, "space", split_axis=1, concat_axis=0, tiled=True)
+        gains.append(slopes(spec, lat_fore, mix, bias))
+    forcing = observe(received, fields, decoder)
+    forcing = lax.all_to_all(forcing, "lead", split_axis=0, concat_axis=0, tiled=True)
+    forcing = lax.all_gather(forcing, "space", axis=1, tiled=True)
+    gain = lax.all_to_all(jnp.stack(gains), "lead", split_axis=0, concat_axis=0, tiled=True)
+
+    incoming = jnp.zeros((width, lat_local * tiles, lon_len), jnp.bfloat16)
+    results = []
+    for section in range(sections - 1, -1, -1):
+        incoming = adjoint_step(
+            incoming,
+            gain[section],
+            forcing[section],
+            decoder_own,
+            outer,
+            inner,
+            lon_back,
+            lat_back,
+            lat_ret,
+            lon_fore.T,
+        )
+        results.append(lax.all_to_all(incoming, "space", split_axis=1, concat_axis=0, tiled=True))
+    grouped = jnp.stack(results[::-1], 0)
+    moved = lax.all_to_all(grouped, "lead", split_axis=0, concat_axis=0, tiled=True)
+    return jnp.transpose(moved, (0, 2, 3, 1))[None]
 
 
 def shards(
@@ -75,6 +322,30 @@
     fields = states[0]
     member_count, lat_local, lon_len, channels = fields.shape
     tiles = lax.axis_size("space")
+    block_total = block_dest.shape[1]
+    slot_cap = 2 * ((block_total + tiles - 1) // tiles)
+    live_rows = lax.broadcasted_iota(jnp.int32, (block_total, OBS_BLK), 1) < block_count[0][:, None]
+    weight_rows = jnp.where(live_rows, obs_weight[0].reshape(block_total, OBS_BLK), 0.0)
+    index_rows = obs_index[0].reshape(block_total, OBS_BLK).astype(jnp.float32)
+    value_rows = jnp.swapaxes(obs_value[0].reshape(member_count, block_total, OBS_BLK), 0, 1)
+    payload = jnp.concatenate([weight_rows[:, None], index_rows[:, None], value_rows], axis=1)
+    targets = block_dest[0]
+    matches = (targets[:, None] == lax.broadcasted_iota(jnp.int32, (block_total, tiles), 1)).astype(
+        jnp.int32
+    )
+    earlier = jnp.cumsum(matches, axis=0) - matches
+    slot_rank = jnp.sum(earlier * matches, axis=1)
+    positions = targets * slot_cap + slot_rank
+    outbox = (
+        jnp.zeros((tiles * slot_cap, member_count + 2, OBS_BLK), jnp.float32)
+        .at[positions]
+        .set(payload)
+    )
+    received = lax.all_to_all(outbox, "space", split_axis=0, concat_axis=0, tiled=True)
+    share_one = member_count == lax.axis_size("lead")
+    aligned = lon_len % 128 == 0 and decoder.shape[1] % 128 == 0 and filter_in.shape[2] % 16 == 0
+    if filter_in.shape[1] == tiles and share_one and aligned:
+        return channel_plan(fields, filter_in, filter_out, filter_bias, decoder, received)
     lon_cos, lon_sin, back_cos, back_sin, lat_cos, lat_sin = make_tables(lon_len, lat_local * tiles)
     spec_re = contract("mfnc,nk->mfkc", fields, lon_cos).astype(jnp.bfloat16)
     spec_im = contract("mfnc,nk->mfkc", fields, lon_sin).astype(jnp.bfloat16)
@@ -90,26 +361,6 @@
     pre_im = block_mix(mode_re, filter_in[1]) + block_mix(mode_im, filter_in[0]) + filter_bias[1]
     slope_re = gelu_slope(pre_re)
     slope_im = gelu_slope(pre_im)
-    block_total = block_dest.shape[1]
-    slot_cap = 2 * ((block_total + tiles - 1) // tiles)
-    live_rows = lax.broadcasted_iota(jnp.int32, (block_total, OBS_BLK), 1) < block_count[0][:, None]
-    weight_rows = jnp.where(live_rows, obs_weight[0].reshape(block_total, OBS_BLK), 0.0)
-    index_rows = obs_index[0].reshape(block_total, OBS_BLK).astype(jnp.float32)
-    value_rows = jnp.swapaxes(obs_value[0].reshape(member_count, block_total, OBS_BLK), 0, 1)
-    payload = jnp.concatenate([weight_rows[:, None], index_rows[:, None], value_rows], axis=1)
-    targets = block_dest[0]
-    matches = (targets[:, None] == lax.broadcasted_iota(jnp.int32, (block_total, tiles), 1)).astype(
-        jnp.int32
-    )
-    earlier = jnp.cumsum(matches, axis=0) - matches
-    slot_rank = jnp.sum(earlier * matches, axis=1)
-    positions = targets * slot_cap + slot_rank
-    outbox = (
-        jnp.zeros((tiles * slot_cap, member_count + 2, OBS_BLK), jnp.float32)
-        .at[positions]
-        .set(payload)
-    )
-    received = lax.all_to_all(outbox, "space", split_axis=0, concat_axis=0, tiled=True)
     got_weight = received[:, 0].reshape(-1)
     got_index = received[:, 1].reshape(-1).astype(jnp.int32)
     got_value = jnp.swapaxes(received[:, 2:], 0, 1).reshape(member_count, -1)

time: 1430 us -> 872 us (0.61)
  local copies, waits for them, and re-layouts: 383 us -> 73 us
  starting transfers between devices: 263 us -> 57.6 us
  Pallas kernels: 0 us -> 204 us
  other arithmetic: 202 us -> 18.8 us
  matrix products: 168 us -> 15.1 us
  waiting for transfers between devices: 329 us -> 413 us
    all_to_all x21 -> x10, starting transfers between devices: 255 us -> 50.3 us  [the longest x4 25.3 us: channel_plan(): lax.all_to_all(spec, 'space', split_axis=1, concat_axis=0, tiled=True)]
    pallas_call x0 -> x9, Pallas kernels: none -> 204 us  [the longest x4 103 us: adjoint_step(): pl.pallas_call(adjoint_kernel, out_shape=jax.ShapeDtypeStruct(incoming.sh...]
    dot_general x92 -> x5, matrix products: 168 us -> 15.1 us  [contract(): jnp.einsum(pattern, left_op, right_op, preferred_element_type=jnp.float32)]
    scatter-add x3 -> x0, other arithmetic: 129 us -> none  [shards(): jnp.zeros_like(decoded).at[:, got_index].add(innovation)]
    gather x2, local copies, waits for them, and re-layouts: 122 us -> 1.35 us  [channel_plan(): jnp.repeat(bias_own.T, lon_len // 2, axis=1, total_repeat_length=lon_len)]
    all_to_all x21 -> x10, waiting for transfers between devices: 327 us -> 413 us  [the longest x4 202 us: channel_plan(): lax.all_to_all(spec, 'space', split_axis=1, concat_axis=0, tiled=True)]
    reshape x4 -> x0, local copies, waits for them, and re-layouts: 78.7 us -> none  [the longest x1 33.7 us: shards(): contract('mfnc,cv->mfnv', fields, decoder).reshape(member_count, -1)]
    convert_element_type x4 -> x5, other arithmetic: 55.8 us -> 2.19 us  [the longest x1 1.35 us: observe(): low = (decoded - high.astype(jnp.float32)).astype(jnp.bfloat16)]
  transfers between devices with their start and end apart: 22 -> 12, of which waited for: 21 -> 10; matrix products, arithmetic and copies ran while one was open for 41% -> 8% of each run, Pallas kernels for 0% -> 7%
where the time goes in v1:
time: 872 us; the launch traced here: 870 us
  waiting for transfers between devices  413 us (47%)
  Pallas kernels  204 us (23%)
  blocking collectives  74.3 us (9%)
  local copies, waits for them, and re-layouts  73 us (8%)
  starting transfers between devices  57.6 us (7%)
  other arithmetic  18.8 us (2%)
  matrix products  15.1 us (2%)
  between operations  13.6 us (2%)
    all_to_all x4, waiting for transfers between devices, channel_plan(): lax.all_to_all(spec, 'space', split_axis=1, concat_axis=0, tiled=True)  202 us
    all_to_all x4, waiting for transfers between devices, channel_plan(): lax.all_to_all(incoming, 'space', split_axis=1, concat_axis=0, tiled=True)  134 us
    pallas_call x4, Pallas kernels, adjoint_step(): pl.pallas_call(adjoint_kernel, out_shape=jax.ShapeDtypeStruct(incoming.sh...  103 us
    all_to_all x1, blocking collectives, channel_plan(): lax.all_to_all(grouped, 'lead', split_axis=0, concat_axis=0, tiled=True)  74.3 us
    all_to_all x1, waiting for transfers between devices, channel_plan(): lax.all_to_all(jnp.stack(gains), 'lead', split_axis=0, concat_axis=0, til...  66.7 us
    pallas_call x4, Pallas kernels, slopes(): pl.pallas_call(slope_kernel, out_shape=jax.ShapeDtypeStruct(spec.shape, j...  58.7 us
    pallas_call x1, Pallas kernels, observe(): pl.pallas_call(observe_kernel, grid=(count // chunk,), in_specs=[pl.Block...  42.5 us
    all_to_all x4, starting transfers between devices, channel_plan(): lax.all_to_all(spec, 'space', split_axis=1, concat_axis=0, tiled=True)  25.3 us
  transfers between devices with their start and end apart: 12, of which 10 were waited for; matrix products, arithmetic and copies ran while one was open for 8% of the time, Pallas kernels for 7%

profile of v1, /device:TPU:0, one launch (start us, length us, event | category | flops | bytes accessed | tf_op | source)
XLA Modules:
  0.0 869.6 jit_solution(9454364344879393865)
XLA Ops:
  15.5 7.3 all-to-all-start.5
  34.1 42.5 %observe.1 = bf16[4,8,128,128]{3,2,1,0:T(8,128)(2,1)} custom-call(s32[1,8192]{1,0:T(1,128)} %and_select_fusion.1.cell_ref, s32[1,8192]{1,0:T(1,128)} %get-tuple-element.17.level_ref, f32[5,8192]{1,0:T(8,128)} %pad_maximum_fusion.2.row_ref, bf16[512,1024]{1,0:T(8,128)(2,1)} %bitcast.189, bf16[512,1024]{1,0:T(8,128)(2,1)} %fusion.2.low_ref), custom_call_target="tpu_custom_call" | custom-call | flops 34359738368 | bytes 4194304 | tf_op jit(solution)/shard_map/observe/pallas_call | solution.py:139
  84.2 10.3 %all-to-all-done.6 = bf16[4,8,128,128]{3,2,1,0:T(8,128)(2,1)S(1)} async-done(((bf16[4,8,128,128]{3,2,1,0:T(8,128)(2,1)}), bf16[4,8,128,128]{3,2,1,0:T(8,128)(2,1)S(1)}, u32[]{:S(2)}, u32[]{:S(2)}) %all-to-all-start.6) | async-done | bytes 1048608 | tf_op jit(solution)/shard_map/all_to_all | solution.py:285
  106.3 59.1 %all-to-all-done = bf16[8,768,128]{2,0,1:T(8,128)(2,1)S(1)} async-done(((bf16[8,768,128]{2,0,1:T(8,128)(2,1)}), bf16[8,768,128]{2,0,1:T(8,128)(2,1)S(1)}, u32[]{:S(2)}, u32[]{:S(2)}) %all-to-all-start) | async-done | bytes 1572896 | tf_op jit(solution)/shard_map/all_to_all | solution.py:282
  176.7 67.3 %all-to-all-done.1 = bf16[8,768,128]{2,0,1:T(8,128)(2,1)S(1)} async-done(((bf16[8,768,128]{2,0,1:T(8,128)(2,1)}), bf16[8,768,128]{2,0,1:T(8,128)(2,1)S(1)}, u32[]{:S(2)}, u32[]{:S(2)}) %all-to-all-start.1) | async-done | bytes 1572896 | tf_op jit(solution)/shard_map/all_to_all | solution.py:282
  244.0 9.6 %all-to-all-start.2 = ((bf16[8,768,128]{2,0,1:T(8,128)(2,1)}), bf16[8,768,128]{2,0,1:T(8,128)(2,1)}, u32[]{:S(2)}, u32[]{:S(2)}) async-start(bf16[8,768,128]{2,0,1:T(8,128)(2,1)} %copy.120), calls=%async_computation.2 | async-start | bytes 3145728 | tf_op jit(solution)/shard_map/all_to_all | solution.py:282
  259.6 49.6 %all-to-all-done.2 = bf16[8,768,128]{2,0,1:T(8,128)(2,1)} async-done(((bf16[8,768,128]{2,0,1:T(8,128)(2,1)}), bf16[8,768,128]{2,0,1:T(8,128)(2,1)}, u32[]{:S(2)}, u32[]{:S(2)}) %all-to-all-start.2) | async-done | bytes 1572896 | tf_op jit(solution)/shard_map/all_to_all | solution.py:282
  324.8 26.2 %all-to-all-done.3 = bf16[8,768,128]{2,0,1:T(8,128)(2,1)} async-done(((bf16[8,768,128]{2,0,1:T(8,128)(2,1)}), bf16[8,768,128]{2,0,1:T(8,128)(2,1)}, u32[]{:S(2)}, u32[]{:S(2)}) %all-to-all-start.3) | async-done | bytes 1572896 | tf_op jit(solution)/shard_map/all_to_all | solution.py:282
  353.8 14.6 %slopes.4 = bf16[64,96,128]{2,1,0:T(8,128)(2,1)} custom-call(bf16[64,96,128]{2,1,0:T(8,128)(2,1)} %bitcast.173, bf16[64,128]{1,0:T(8,128)(2,1)} %get-tuple-element.34.lat_ref.fore_ref, bf16[96,192]{1,0:T(8,128)(2,1)} %copy.115.mix_ref, f32[96,128]{1,0:T(8,128)} %bitcast.185), custom_call_target="tpu_custom_call" | custom-call | flops 503316480 | bytes 3145728 | tf_op jit(solution)/shard_map/slopes/pallas_call | solution.py:183
  368.5 14.6 %slopes.5 = bf16[64,96,128]{2,1,0:T(8,128)(2,1)} custom-call(bf16[64,96,128]{2,1,0:T(8,128)(2,1)} %bitcast.174, bf16[64,128]{1,0:T(8,128)(2,1)} %get-tuple-element.34.lat_ref.fore_ref, bf16[96,192]{1,0:T(8,128)(2,1)} %copy.115.mix_ref, f32[96,128]{1,0:T(8,128)} %bitcast.186), custom_call_target="tpu_custom_call" | custom-call | flops 503316480 | bytes 3145728 | tf_op jit(solution)/shard_map/slopes/pallas_call | solution.py:183
  383.1 14.7 %slopes.6 = bf16[64,96,128]{2,1,0:T(8,128)(2,1)} custom-call(bf16[64,96,128]{2,1,0:T(8,128)(2,1)} %bitcast.175, bf16[64,128]{1,0:T(8,128)(2,1)} %get-tuple-element.34.lat_ref.fore_ref, bf16[96,192]{1,0:T(8,128)(2,1)} %copy.115.mix_ref, f32[96,128]{1,0:T(8,128)} %bitcast.187), custom_call_target="tpu_custom_call" | custom-call | flops 503316480 | bytes 3145728 | tf_op jit(solution)/shard_map/slopes/pallas_call | solution.py:183
  397.8 14.8 %slopes.7 = bf16[64,96,128]{2,1,0:T(8,128)(2,1)} custom-call(bf16[64,96,128]{2,1,0:T(8,128)(2,1)} %bitcast.179, bf16[64,128]{1,0:T(8,128)(2,1)} %get-tuple-element.34.lat_ref.fore_ref, bf16[96,192]{1,0:T(8,128)(2,1)} %copy.115.mix_ref, f32[96,128]{1,0:T(8,128)} %bitcast.188), custom_call_target="tpu_custom_call" | custom-call | flops 503316480 | bytes 3145728 | tf_op jit(solution)/shard_map/slopes/pallas_call | solution.py:183
  426.9 66.7 %all-to-all-done.4 = bf16[4,64,96,128]{3,2,1,0:T(8,128)(2,1)} async-done(((bf16[4,64,96,128]{3,2,1,0:T(8,128)(2,1)}), bf16[4,64,96,128]{3,2,1,0:T(8,128)(2,1)}, u32[]{:S(2)}, u32[]{:S(2)}) %all-to-all-start.4) | async-done | bytes 6291488 | tf_op jit(solution)/shard_map/all_to_all | solution.py:287
  493.6 6.1 slice_bitcast_fusion.4
  507.3 25.7 %adjoint.4.in_ref = bf16[96,64,128]{2,1,0:T(8,128)(2,1)} custom-call(bf16[96,64,128]{2,1,0:T(8,128)(2,1)} %broadcast_in_dim.32.in_ref, bf16[64,96,128]{2,1,0:T(8,128)(2,1)} %get-tuple-element.28.gain_ref, bf16[64,128,128]{2,1,0:T(8,128)(2,1)} %get-tuple-element.24.level_ref, bf16[96,128]{1,0:T(8,128)(2,1)} %constant_dynamic-slice_fusion.decoder_ref, ...), custom_call_target="tpu_custom_call" | custom-call | flops 1811939328 | bytes 7864320 | tf_op jit(solution)/shard_map/adjoint/pallas_call | solution.py:241
  533.0 25.6 %adjoint.5.in_ref = bf16[96,64,128]{2,1,0:T(8,128)(2,1)} custom-call(bf16[96,64,128]{2,1,0:T(8,128)(2,1)} %adjoint.4.in_ref, bf16[64,96,128]{2,1,0:T(8,128)(2,1)} %get-tuple-element.27.gain_ref, bf16[64,128,128]{2,1,0:T(8,128)(2,1)} %get-tuple-element.23.level_ref, bf16[96,128]{1,0:T(8,128)(2,1)} %constant_dynamic-slice_fusion.decoder_ref, ...), custom_call_target="tpu_custom_call" | custom-call | flops 1811939328 | bytes 7864320 | tf_op jit(solution)/shard_map/adjoint/pallas_call | solution.py:241
  558.6 25.7 %adjoint.6.in_ref = bf16[96,64,128]{2,1,0:T(8,128)(2,1)} custom-call(bf16[96,64,128]{2,1,0:T(8,128)(2,1)} %adjoint.5.in_ref, bf16[64,96,128]{2,1,0:T(8,128)(2,1)} %get-tuple-element.26.gain_ref, bf16[64,128,128]{2,1,0:T(8,128)(2,1)} %get-tuple-element.22.level_ref, bf16[96,128]{1,0:T(8,128)(2,1)} %constant_dynamic-slice_fusion.decoder_ref, ...), custom_call_target="tpu_custom_call" | custom-call | flops 1811939328 | bytes 7864320 | tf_op jit(solution)/shard_map/adjoint/pallas_call | solution.py:241
  584.3 25.6 %adjoint.7 = bf16[96,64,128]{2,1,0:T(8,128)(2,1)} custom-call(bf16[96,64,128]{2,1,0:T(8,128)(2,1)} %adjoint.6.in_ref, bf16[64,96,128]{2,1,0:T(8,128)(2,1)} %get-tuple-element.25.gain_ref, bf16[64,128,128]{2,1,0:T(8,128)(2,1)} %get-tuple-element.21.level_ref, bf16[96,128]{1,0:T(8,128)(2,1)} %constant_dynamic-slice_fusion.decoder_ref, ...), custom_call_target="tpu_custom_call" | custom-call | flops 1811939328 | bytes 7864320 | tf_op jit(solution)/shard_map/adjoint/pallas_call | solution.py:241
  619.4 34.8 %all-to-all-done.7 = bf16[96,64,128]{2,0,1:T(8,128)(2,1)S(1)} async-done(((bf16[96,64,128]{2,0,1:T(8,128)(2,1)}), bf16[96,64,128]{2,0,1:T(8,128)(2,1)S(1)}, u32[]{:S(2)}, u32[]{:S(2)}) %all-to-all-start.7) | async-done | bytes 1572896 | tf_op jit(solution)/shard_map/all_to_all | solution.py:304
  660.9 34.3 %all-to-all-done.8 = bf16[96,64,128]{2,0,1:T(8,128)(2,1)} async-done(((bf16[96,64,128]{2,0,1:T(8,128)(2,1)}), bf16[96,64,128]{2,0,1:T(8,128)(2,1)}, u32[]{:S(2)}, u32[]{:S(2)}) %all-to-all-start.8) | async-done | bytes 1572896 | tf_op jit(solution)/shard_map/all_to_all | solution.py:304
  701.7 34.3 %all-to-all-done.9 = bf16[96,64,128]{2,0,1:T(8,128)(2,1)} async-done(((bf16[96,64,128]{2,0,1:T(8,128)(2,1)}), bf16[96,64,128]{2,0,1:T(8,128)(2,1)}, u32[]{:S(2)}, u32[]{:S(2)}) %all-to-all-start.9) | async-done | bytes 1572896 | tf_op jit(solution)/shard_map/all_to_all | solution.py:304
  746.7 30.2 %all-to-all-done.10 = bf16[96,64,128]{2,0,1:T(8,128)(2,1)S(1)} async-done(((bf16[96,64,128]{2,0,1:T(8,128)(2,1)}), bf16[96,64,128]{2,0,1:T(8,128)(2,1)S(1)}, u32[]{:S(2)}, u32[]{:S(2)}) %all-to-all-start.10) | async-done | bytes 1572896 | tf_op jit(solution)/shard_map/all_to_all | solution.py:304
  779.6 74.3 %all_to_all.152 = bf16[4,768,8,128]{3,2,1,0:T(8,128)(2,1)} all-to-all(bf16[4,768,8,128]{3,2,1,0:T(8,128)(2,1)S(1)} %pad_maximum_fusion.1), channel_id=1, replica_groups=mesh['lead'=4,'space'=8] {'lead'}, dimensions={0} | all-to-all | bytes 12582912 | tf_op jit(solution)/shard_map/all_to_all | solution.py:306
  853.8 9.0 %copy.146 = bf16[1,4,8,128,768]{4,3,2,1,0:T(8,128)(2,1)} copy(bf16[1,4,8,128,768]{3,2,4,1,0:T(8,128)(2,1)} %bitcast.166) | data formatting | bytes 12582912 | tf_op jit(solution)/shard_map/broadcast_in_dim | solution.py:307
  (95 shorter events, 133.3 us)
Async XLA Ops:
  6.5 16.3 %copy-start = (bf16[768,128]{1,0:T(8,128)(2,1)S(1)}, bf16[768,128]{1,0:T(8,128)(2,1)}, u32[]{:S(2)}) copy-start(bf16[768,128]{1,0:T(8,128)(2,1)} %param.16) | copy-start | bytes 589828
  15.5 16.3 %all-to-all-start.5 = ((f32[64,6,128]{2,1,0:T(8,128)}), f32[64,6,128]{2,1,0:T(8,128)S(1)}, u32[]{:S(2)}, u32[]{:S(2)}) async-start(f32[64,6,128]{2,1,0:T(8,128)} %scatter_fusion), calls=%async_computation.5 | async-start | bytes 524288 | tf_op jit(solution)/shard_map/all_to_all | solution.py:344
  76.6 18.0 %all-to-all-start.6 = ((bf16[4,8,128,128]{3,2,1,0:T(8,128)(2,1)}), bf16[4,8,128,128]{3,2,1,0:T(8,128)(2,1)S(1)}, u32[]{:S(2)}, u32[]{:S(2)}) async-start(bf16[4,8,128,128]{3,2,1,0:T(8,128)(2,1)} %observe.1), calls=%async_computation.6 | async-start | bytes 2097152 | tf_op jit(solution)/shard_map/all_to_all | solution.py:285
  94.6 1.0 copy-start.8
  95.6 69.7 %all-to-all-start = ((bf16[8,768,128]{2,0,1:T(8,128)(2,1)}), bf16[8,768,128]{2,0,1:T(8,128)(2,1)S(1)}, u32[]{:S(2)}, u32[]{:S(2)}) async-start(bf16[8,768,128]{2,0,1:T(8,128)(2,1)} %copy.111), calls=%async_computation | async-start | bytes 3145728 | tf_op jit(solution)/shard_map/all_to_all | solution.py:282
  101.6 398.2 %all-gather.2.cloned.1.call-start = ((), (), s32[]{:S(2)}) async-start(), calls=%async_computation.12 | async-start | bytes 9437184 | tf_op jit(solution)/shard_map/all_gather | solution.py:286
  165.3 78.7 %all-to-all-start.1 = ((bf16[8,768,128]{2,0,1:T(8,128)(2,1)}), bf16[8,768,128]{2,0,1:T(8,128)(2,1)S(1)}, u32[]{:S(2)}, u32[]{:S(2)}) async-start(bf16[8,768,128]{2,0,1:T(8,128)(2,1)} %copy.116), calls=%async_computation.1 | async-start | bytes 3145728 | tf_op jit(solution)/shard_map/all_to_all | solution.py:282
  244.0 65.2 %all-to-all-start.2 = ((bf16[8,768,128]{2,0,1:T(8,128)(2,1)}), bf16[8,768,128]{2,0,1:T(8,128)(2,1)}, u32[]{:S(2)}, u32[]{:S(2)}) async-start(bf16[8,768,128]{2,0,1:T(8,128)(2,1)} %copy.120), calls=%async_computation.2 | async-start | bytes 3145728 | tf_op jit(solution)/shard_map/all_to_all | solution.py:282
  259.6 57.1 %copy-start.9 = (s32[128]{0:T(128)S(1)}, s32[128]{0:T(128)}, u32[]{:S(2)}) copy-start(s32[128]{0:T(128)} %constant.184) | copy-start | bytes 1540
  309.1 41.8 %all-to-all-start.3 = ((bf16[8,768,128]{2,0,1:T(8,128)(2,1)}), bf16[8,768,128]{2,0,1:T(8,128)(2,1)}, u32[]{:S(2)}, u32[]{:S(2)}) async-start(bf16[8,768,128]{2,0,1:T(8,128)(2,1)} %copy.124), calls=%async_computation.3 | async-start | bytes 3145728 | tf_op jit(solution)/shard_map/all_to_all | solution.py:282
  397.8 14.8 %copy-start.6 = (bf16[64,96,128]{2,1,0:T(8,128)(2,1)S(1)}, bf16[64,96,128]{2,1,0:T(8,128)(2,1)}, u32[]{:S(2)}) copy-start(bf16[64,96,128]{2,1,0:T(8,128)(2,1)} %slopes.4) | copy-start | bytes 4718596
  397.8 14.8 %copy-start.7 = (bf16[64,96,128]{2,1,0:T(8,128)(2,1)S(1)}, bf16[64,96,128]{2,1,0:T(8,128)(2,1)}, u32[]{:S(2)}) copy-start(bf16[64,96,128]{2,1,0:T(8,128)(2,1)} %slopes.5) | copy-start | bytes 4718596
  417.7 76.0 %all-to-all-start.4 = ((bf16[4,64,96,128]{3,2,1,0:T(8,128)(2,1)}), bf16[4,64,96,128]{3,2,1,0:T(8,128)(2,1)}, u32[]{:S(2)}, u32[]{:S(2)}) async-start(bf16[4,64,96,128]{3,2,1,0:T(8,128)(2,1)} %pad_maximum_fusion), calls=%async_computation.4 | async-start | bytes 12582912 | tf_op jit(solution)/shard_map/all_to_all | solution.py:287
  613.5 3.8 copy-start.3
  613.5 40.7 %all-to-all-start.7 = ((bf16[96,64,128]{2,0,1:T(8,128)(2,1)}), bf16[96,64,128]{2,0,1:T(8,128)(2,1)S(1)}, u32[]{:S(2)}, u32[]{:S(2)}) async-start(bf16[96,64,128]{2,0,1:T(8,128)(2,1)} %copy.134), calls=%async_computation.7 | async-start | bytes 3145728 | tf_op jit(solution)/shard_map/all_to_all | solution.py:304
  619.4 39.3 %copy-start.2 = (bf16[96,64,128]{2,1,0:T(8,128)(2,1)S(1)}, bf16[96,64,128]{2,1,0:T(8,128)(2,1)}, u32[]{:S(2)}) copy-start(bf16[96,64,128]{2,1,0:T(8,128)(2,1)} %adjoint.5.in_ref) | copy-start | bytes 4718596
  654.2 41.0 %all-to-all-start.8 = ((bf16[96,64,128]{2,0,1:T(8,128)(2,1)}), bf16[96,64,128]{2,0,1:T(8,128)(2,1)}, u32[]{:S(2)}, u32[]{:S(2)}) async-start(bf16[96,64,128]{2,0,1:T(8,128)(2,1)} %copy.137), calls=%async_computation.8 | async-start | bytes 3145728 | tf_op jit(solution)/shard_map/all_to_all | solution.py:304
  660.9 38.6 %copy-start.1 = (bf16[96,64,128]{2,1,0:T(8,128)(2,1)S(1)}, bf16[96,64,128]{2,1,0:T(8,128)(2,1)}, u32[]{:S(2)}) copy-start(bf16[96,64,128]{2,1,0:T(8,128)(2,1)} %adjoint.4.in_ref) | copy-start | bytes 4718596
  695.2 40.8 %all-to-all-start.9 = ((bf16[96,64,128]{2,0,1:T(8,128)(2,1)}), bf16[96,64,128]{2,0,1:T(8,128)(2,1)}, u32[]{:S(2)}, u32[]{:S(2)}) async-start(bf16[96,64,128]{2,0,1:T(8,128)(2,1)} %copy.140), calls=%async_computation.9 | async-start | bytes 3145728 | tf_op jit(solution)/shard_map/all_to_all | solution.py:304
  736.0 40.8 %all-to-all-start.10 = ((bf16[96,64,128]{2,0,1:T(8,128)(2,1)}), bf16[96,64,128]{2,0,1:T(8,128)(2,1)S(1)}, u32[]{:S(2)}, u32[]{:S(2)}) async-start(bf16[96,64,128]{2,0,1:T(8,128)(2,1)} %copy.143), calls=%async_computation.10 | async-start | bytes 3145728 | tf_op jit(solution)/shard_map/all_to_all | solution.py:304
  776.8 1.4 copy-start.4
  776.8 1.9 copy-start.5
Sparse Core Ops, SparseCore 0:
  104.6 200.9 all-gather.1

commit v2 on v1

--- a/solution.py
+++ b/solution.py
@@ -2,6 +2,7 @@
 
 import jax
 import jax.numpy as jnp
+import numpy as np
 from jax import lax
 from jax.experimental import pallas as pl
 from jax.experimental.pallas import tpu as pltpu
@@ -48,6 +49,30 @@
     return (lon_cos, lon_sin, back_cos, back_sin, lat_cos, lat_sin)
 
 
+def fixed_tables(lon_len, lat_len):
+    def waves(rows, cols, length):
+        angles = (np.arange(rows)[:, None] * np.arange(cols)[None, :] % length).astype(np.float32)
+        angles = angles * np.float32(2.0 * math.pi / length)
+        return np.cos(angles), np.sin(angles)
+
+    modes = lon_len // 2
+    lon_scale = np.float32(1.0 / math.sqrt(lon_len))
+    lat_scale = np.float32(1.0 / math.sqrt(lat_len))
+    cos, sin = waves(lon_len, modes, lon_len)
+    lon = np.concatenate([cos, -sin], axis=1) * lon_scale
+    factor = np.where(np.arange(2 * modes) % modes == 0, 1.0, 2.0).astype(np.float32)
+    lat_cos, lat_sin = (part * lat_scale for part in waves(lat_len, lat_len, lat_len))
+    found = (
+        lon,
+        lon * factor,
+        np.concatenate([lat_cos, lat_sin], axis=1),
+        np.concatenate([lat_cos.T, lat_sin.T], axis=1),
+        np.concatenate([lat_cos.T, -lat_sin.T], axis=1),
+        lon.T,
+    )
+    return tuple(jnp.asarray(table.astype(jnp.bfloat16)) for table in found)
+
+
 def contract(pattern, left_op, right_op):
     return jnp.einsum(pattern, left_op, right_op, preferred_element_type=jnp.float32)
 
@@ -78,6 +103,10 @@
     lanes = lax.broadcasted_iota(jnp.int32, values.shape, 1)
     rolled = pltpu.roll(values, half, 1)
     return jnp.where(lanes < half, rolled, -rolled)
+
+
+def tied(value, *others):
+    return lax.optimization_barrier((value,) + others)[0]
 
 
 def doubled(values):
@@ -159,6 +188,44 @@
     )(index // levels, index % levels, rows, high, low)
 
 
+def spectrum_kernel(which_ref, state_ref, table_ref, *rest):
+    out_ref = rest[-1]
+    parts, _, width, waves = out_ref.shape
+    dims = (((0,), (0,)), ((), ()))
+    spec = lax.dot_general(
+        state_ref[0, 0], table_ref[...], dims, preferred_element_type=jnp.float32
+    )
+    out_ref[:, 0] = spec.reshape(parts, width, waves).astype(jnp.bfloat16)
+
+
+def spectrum_of(fields, which, table, parts, *before):
+    members, lats, lons, channels = fields.shape
+    width = channels // parts
+    waves = table.shape[1]
+    spec = pltpu.PrefetchScalarGridSpec(
+        num_scalar_prefetch=1,
+        grid=(lats,),
+        in_specs=[
+            pl.BlockSpec((1, 1, lons, channels), lambda f, which_ref: (which_ref[0], f, 0, 0)),
+            pl.BlockSpec((lons, waves), lambda f, which_ref: (0, 0)),
+        ]
+        + [pl.BlockSpec(memory_space=pl.ANY)] * len(before),
+        out_specs=pl.BlockSpec((parts, 1, width, waves), lambda f, which_ref: (0, f, 0, 0)),
+    )
+    return pl.pallas_call(
+        spectrum_kernel,
+        grid_spec=spec,
+        out_shape=jax.ShapeDtypeStruct((parts, lats, width, waves), jnp.bfloat16),
+        compiler_params=pltpu.CompilerParams(vmem_limit_bytes=VMEM_BYTES),
+        cost_estimate=pl.CostEstimate(
+            flops=2 * lats * lons * channels * waves,
+            bytes_accessed=4 * lats * lons * channels,
+            transcendentals=0,
+        ),
+        name="spectrum",
+    )(which.reshape(1), fields, table, *before)
+
+
 def slope_kernel(spec_ref, lat_ref, mix_ref, bias_ref, out_ref, hold):
     lats, width, waves = spec_ref.shape
 
@@ -261,12 +328,9 @@
     sections = lax.axis_size("lead")
     me = lax.axis_index("space")
     width = filter_in.shape[2]
-    lon_cos, lon_sin, back_cos, back_sin, lat_cos, lat_sin = make_tables(lon_len, lat_local * tiles)
-    lon_fore = jnp.concatenate([lon_cos, lon_sin], axis=1)
-    lon_back = jnp.concatenate([back_cos, back_sin], axis=0).T
-    lat_fore = jnp.concatenate([lat_cos, lat_sin], axis=1)
-    lat_back = jnp.concatenate([lat_cos.T, lat_sin.T], axis=1)
-    lat_ret = jnp.concatenate([lat_cos.T, -lat_sin.T], axis=1)
+    lon_fore, lon_back, lat_fore, lat_back, lat_ret, lon_lift = fixed_tables(
+        lon_len, lat_local * tiles
+    )
     first = lax.dynamic_index_in_dim(filter_in, me, 1, keepdims=False)
     second = lax.dynamic_index_in_dim(filter_out, me, 1, keepdims=False)
     mix = jnp.concatenate([first[0].T, -first[1].T], axis=1)
@@ -276,33 +340,73 @@
     bias = jnp.repeat(bias_own.T, lon_len // 2, axis=1, total_repeat_length=lon_len)
     decoder_own = lax.dynamic_slice_in_dim(decoder, me * width, width, 0)
 
-    gains = []
-    for m in range(member_count):
-        spec = contract("fnc,nk->fck", fields[m], lon_fore).astype(jnp.bfloat16)
-        spec = lax.all_to_all(spec, "space", split_axis=1, concat_axis=0, tiled=True)
-        gains.append(slopes(spec, lat_fore, mix, bias))
-    forcing = observe(received, fields, decoder)
-    forcing = lax.all_to_all(forcing, "lead", split_axis=0, concat_axis=0, tiled=True)
-    forcing = lax.all_gather(forcing, "space", axis=1, tiled=True)
-    gain = lax.all_to_all(jnp.stack(gains), "lead", split_axis=0, concat_axis=0, tiled=True)
+    turns = [t for t in range(1, sections)] + [0]
+    turns = turns[1:2] + turns[:1] + turns[2:]
+    lead = lax.axis_index("lead")
+
+    def own_index(turn):
+        return lax.rem(lead + turn, sections)
+
+    def hand_over(piece, turn):
+        if turn == 0:
+            return piece
+        return lax.ppermute(piece, "lead", [(i, (i + turn) % sections) for i in range(sections)])
+
+    def section_of(arrived, section):
+        stacked = jnp.stack([arrived[t] for t in range(sections)])
+        return lax.dynamic_index_in_dim(
+            stacked, lax.rem(lead + sections - section, sections), 0, keepdims=False
+        )
+
+    gains = {}
+    level_parts = {}
+    made = []
+    for order, turn in enumerate(turns):
+        before = ()
+        if order == 1:
+            before = (forcing,)
+        if order > 1:
+            before = (made[order - 2],)
+        spec = spectrum_of(fields, own_index(turn), lon_fore, tiles, *before)
+        spec = lax.all_to_all(spec, "space", split_axis=0, concat_axis=0, tiled=True)
+        spec = spec.reshape((-1,) + spec.shape[2:])
+        if order == 0:
+            forcing = observe(received, fields, decoder)
+        if order == sections - 1:
+            last_spec = spec
+        made.append(slopes(spec, lat_fore, mix, bias))
+        gains[turn] = hand_over(made[-1], turn)
+    for turn in turns:
+        piece = lax.dynamic_index_in_dim(forcing, own_index(turn), 0, keepdims=False)
+        level_parts[turn] = hand_over(piece, turn)
+    levels = [section_of(level_parts, section) for section in range(sections)]
+    top = sections - 1
+    top_level = lax.all_gather(tied(levels[top], last_spec), "space", axis=0, tiled=True)
+    rest = lax.all_gather(
+        tied(jnp.stack(levels[:top]), last_spec), "space", axis=1, tiled=True
+    )
 
     incoming = jnp.zeros((width, lat_local * tiles, lon_len), jnp.bfloat16)
-    results = []
-    for section in range(sections - 1, -1, -1):
+    results = {}
+    for section in range(top, -1, -1):
+        if section + 2 in results:
+            incoming = tied(incoming, results[section + 2])
         incoming = adjoint_step(
             incoming,
-            gain[section],
-            forcing[section],
+            section_of(gains, section),
+            top_level if section == top else rest[section],
             decoder_own,
             outer,
             inner,
             lon_back,
             lat_back,
             lat_ret,
-            lon_fore.T,
-        )
-        results.append(lax.all_to_all(incoming, "space", split_axis=1, concat_axis=0, tiled=True))
-    grouped = jnp.stack(results[::-1], 0)
+            lon_lift,
+        )
+        results[section] = lax.all_to_all(
+            incoming, "space", split_axis=1, concat_axis=0, tiled=True
+        )
+    grouped = jnp.stack([results[section] for section in range(sections)], 0)
     moved = lax.all_to_all(grouped, "lead", split_axis=0, concat_axis=0, tiled=True)
     return jnp.transpose(moved, (0, 2, 3, 1))[None]
 

time: 872 us -> 685 us (0.79)
  waiting for transfers between devices: 413 us -> 185 us
  blocking collectives: 74.3 us -> 137 us
  Pallas kernels: 204 us -> 229 us
  local copies, waits for them, and re-layouts: 73 us -> 55.2 us
  starting transfers between devices: 57.6 us -> 42.7 us
  matrix products: 15.1 us -> 4.96 us
    all_to_all x6 -> x3, waiting for transfers between devices: 279 us -> 119 us  [channel_plan(): lax.all_to_all(spec, 'space', split_axis=0, concat_axis=0, tiled=True)]
    all_to_all x4, waiting for transfers between devices: 134 us -> 51.4 us  [channel_plan(): lax.all_to_all(incoming, 'space', split_axis=1, concat_axis=0, tiled=True)]
    all_to_all x0 -> x1, blocking collectives: none -> 63.2 us  [channel_plan(): lax.all_to_all(spec, 'space', split_axis=0, concat_axis=0, tiled=True)]
    pallas_call x0 -> x4, Pallas kernels: none -> 25.1 us  [spectrum_of(): pl.pallas_call(spectrum_kernel, grid_spec=spec, out_shape=jax.ShapeDtypeS...]
    all_to_all x6 -> x3, starting transfers between devices: 34.1 us -> 14.5 us  [channel_plan(): lax.all_to_all(spec, 'space', split_axis=0, concat_axis=0, tiled=True)]
    ppermute x0 -> x6, waiting for transfers between devices: none -> 14.3 us  [hand_over(): lax.ppermute(piece, 'lead', [(i, (i + turn) % sections) for i in range(se...]
    dot_general x5 -> x1, matrix products: 15.1 us -> 4.96 us  [contract(): jnp.einsum(pattern, left_op, right_op, preferred_element_type=jnp.float32)]
    convert_element_type x4 -> x0, local copies, waits for them, and re-layouts: 9.81 us -> none  [channel_plan(): spec = contract('fnc,nk->fck', fields[m], lon_fore).astype(jnp.bfloat16)]
  transfers between devices with their start and end apart: 12 -> 16, of which waited for: 10 -> 11; matrix products, arithmetic and copies ran while one was open for 8% -> 7% of each run, Pallas kernels for 7% -> 23%
where the time goes in v2:
time: 685 us; the launch traced here: 683 us
  Pallas kernels  229 us (33%)
  waiting for transfers between devices  185 us (27%)
  blocking collectives  137 us (20%)
  local copies, waits for them, and re-layouts  55.2 us (8%)
  starting transfers between devices  42.7 us (6%)
  other arithmetic  15.3 us (2%)
  between operations  13.6 us (2%)
    all_to_all x3, waiting for transfers between devices, channel_plan(): lax.all_to_all(spec, 'space', split_axis=0, concat_axis=0, tiled=True)  119 us
    pallas_call x4, Pallas kernels, adjoint_step(): pl.pallas_call(adjoint_kernel, out_shape=jax.ShapeDtypeStruct(incoming.sh...  103 us
    all_to_all x1, blocking collectives, channel_plan(): lax.all_to_all(grouped, 'lead', split_axis=0, concat_axis=0, tiled=True)  74.3 us
    all_to_all x1, blocking collectives, channel_plan(): lax.all_to_all(spec, 'space', split_axis=0, concat_axis=0, tiled=True)  63.2 us
    pallas_call x4, Pallas kernels, slopes(): pl.pallas_call(slope_kernel, out_shape=jax.ShapeDtypeStruct(spec.shape, j...  58.5 us
    all_to_all x4, waiting for transfers between devices, channel_plan(): lax.all_to_all(incoming, 'space', split_axis=1, concat_axis=0, tiled=True)  51.4 us
    pallas_call x1, Pallas kernels, observe(): pl.pallas_call(observe_kernel, grid=(count // chunk,), in_specs=[pl.Block...  42.5 us
    pallas_call x4, Pallas kernels, spectrum_of(): pl.pallas_call(spectrum_kernel, grid_spec=spec, out_shape=jax.ShapeDtypeS...  25.1 us
  transfers between devices with their start and end apart: 16, of which 11 were waited for; matrix products, arithmetic and copies ran while one was open for 7% of the time, Pallas kernels for 23%

profile of v2, /device:TPU:0, one launch (start us, length us, event | category | flops | bytes accessed | tf_op | source)
XLA Modules:
  0.0 682.6 jit_solution(14897794022369656279)
XLA Ops:
  15.6 7.3 %all-to-all-start = ((f32[64,6,128]{2,1,0:T(8,128)}), f32[64,6,128]{2,1,0:T(8,128)S(1)}, u32[]{:S(2)}, u32[]{:S(2)}) async-start(f32[64,6,128]{2,1,0:T(8,128)} %scatter_fusion), calls=%async_computation | async-start | bytes 524288 | tf_op jit(solution)/shard_map/all_to_all | solution.py:448
  34.2 42.5 %observe.1.rest_0_ = bf16[4,8,128,128]{3,2,1,0:T(8,128)(2,1)} custom-call(s32[1,8192]{1,0:T(1,128)} %and_select_fusion.1.cell_ref, s32[1,8192]{1,0:T(1,128)} %get-tuple-element.21.level_ref, f32[5,8192]{1,0:T(8,128)} %pad_maximum_fusion.4.row_ref, bf16[512,1024]{1,0:T(8,128)(2,1)} %bitcast.146, bf16[512,1024]{1,0:T(8,128)(2,1)} %fusion.low_ref), custom_call_target="tpu_custom_call" | custom-call | flops 34359738368 | bytes 4194304 | tf_op jit(solution)/shard_map/observe/pallas_call | solution.py:168
  76.7 6.2 spectrum.4
  93.4 32.1 %all-to-all-done.1 = bf16[8,8,96,128]{3,2,1,0:T(8,128)(2,1)S(1)} async-done(((bf16[8,8,96,128]{3,2,1,0:T(8,128)(2,1)}), bf16[8,8,96,128]{3,2,1,0:T(8,128)(2,1)S(1)}, u32[]{:S(2)}, u32[]{:S(2)}) %all-to-all-start.1) | async-done | bytes 1572896 | tf_op jit(solution)/shard_map/all_to_all | solution.py:371
  126.6 14.6 %slopes.4.rest_0_ = bf16[64,96,128]{2,1,0:T(8,128)(2,1)} custom-call(bf16[64,96,128]{2,1,0:T(8,128)(2,1)} %bitcast.133, bf16[64,128]{1,0:T(8,128)(2,1)} %constant.207.clone.lat_ref.fore_ref, bf16[96,192]{1,0:T(8,128)(2,1)} %copy.64.mix_ref, f32[96,128]{1,0:T(8,128)} %bitcast.142), custom_call_target="tpu_custom_call" | custom-call | flops 503316480 | bytes 3145728 | tf_op jit(solution)/shard_map/slopes/pallas_call | solution.py:250
  141.3 6.2 spectrum.5
  159.9 6.8 collective-permute-done.4
  167.7 20.8 %all-to-all-done.2 = bf16[8,8,96,128]{3,2,1,0:T(8,128)(2,1)S(1)} async-done(((bf16[8,8,96,128]{3,2,1,0:T(8,128)(2,1)}), bf16[8,8,96,128]{3,2,1,0:T(8,128)(2,1)S(1)}, u32[]{:S(2)}, u32[]{:S(2)}) %all-to-all-start.2) | async-done | bytes 1572896 | tf_op jit(solution)/shard_map/all_to_all | solution.py:371
  189.7 6.3 spectrum.6
  196.0 63.2 %all_to_all.90 = bf16[8,8,96,128]{3,2,1,0:T(8,128)(2,1)} all-to-all(bf16[8,8,96,128]{3,2,1,0:T(8,128)(2,1)} %spectrum.6), channel_id=1, replica_groups=mesh['lead'=4,'space'=8] {'space'}, dimensions={0} | all-to-all | bytes 3145728 | tf_op jit(solution)/shard_map/all_to_all | solution.py:371
  259.1 14.6 %slopes.6.rest_0_ = bf16[64,96,128]{2,1,0:T(8,128)(2,1)} custom-call(bf16[64,96,128]{2,1,0:T(8,128)(2,1)} %bitcast.140, bf16[64,128]{1,0:T(8,128)(2,1)} %constant.207.clone.lat_ref.fore_ref, bf16[96,192]{1,0:T(8,128)(2,1)} %copy.64.mix_ref, f32[96,128]{1,0:T(8,128)} %bitcast.143), custom_call_target="tpu_custom_call" | custom-call | flops 503316480 | bytes 3145728 | tf_op jit(solution)/shard_map/slopes/pallas_call | solution.py:250
  273.7 6.3 spectrum.7
  286.2 66.2 %all-to-all-done.4 = bf16[8,8,96,128]{3,2,1,0:T(8,128)(2,1)} async-done(((bf16[8,8,96,128]{3,2,1,0:T(8,128)(2,1)}), bf16[8,8,96,128]{3,2,1,0:T(8,128)(2,1)}, u32[]{:S(2)}, u32[]{:S(2)}) %all-to-all-start.4) | async-done | bytes 1572896 | tf_op jit(solution)/shard_map/all_to_all | solution.py:371
  352.3 14.6 %slopes.7 = bf16[64,96,128]{2,1,0:T(8,128)(2,1)} custom-call(bf16[64,96,128]{2,1,0:T(8,128)(2,1)} %bitcast.34.spec_ref, bf16[64,128]{1,0:T(8,128)(2,1)} %constant.207.clone.lat_ref.fore_ref, bf16[96,192]{1,0:T(8,128)(2,1)} %copy.64.mix_ref, f32[96,128]{1,0:T(8,128)} %bitcast.144), custom_call_target="tpu_custom_call" | custom-call | flops 503316480 | bytes 3145728 | tf_op jit(solution)/shard_map/slopes/pallas_call | solution.py:250
  369.2 14.6 %slopes.5 = bf16[64,96,128]{2,1,0:T(8,128)(2,1)} custom-call(bf16[64,96,128]{2,1,0:T(8,128)(2,1)} %bitcast.131, bf16[64,128]{1,0:T(8,128)(2,1)} %constant.207.clone.lat_ref.fore_ref, bf16[96,192]{1,0:T(8,128)(2,1)} %copy.64.mix_ref, f32[96,128]{1,0:T(8,128)} %bitcast.145), custom_call_target="tpu_custom_call" | custom-call | flops 503316480 | bytes 3145728 | tf_op jit(solution)/shard_map/slopes/pallas_call | solution.py:250
  393.4 25.6 %adjoint.4.in_ref = bf16[96,64,128]{2,1,0:T(8,128)(2,1)} custom-call(bf16[96,64,128]{2,1,0:T(8,128)(2,1)} %broadcast_in_dim.24.in_ref, bf16[64,96,128]{2,1,0:T(8,128)(2,1)} %get-tuple-element.31.gain_ref, bf16[64,128,128]{2,1,0:T(8,128)(2,1)} %all-gather.3.cloned.1.call-done.level_ref, bf16[96,128]{1,0:T(8,128)(2,1)} %constant_dynamic-slice_fusion.3.decoder_ref, ...), custom_call_target="tpu_custom_call" | custom-call | flops 1811939328 | bytes 7864320 | tf_op jit(solution)/shard_map/adjoint/pallas_call | solution.py:308
  433.5 25.7 %adjoint.5.in_ref = bf16[96,64,128]{2,1,0:T(8,128)(2,1)} custom-call(bf16[96,64,128]{2,1,0:T(8,128)(2,1)} %adjoint.4.in_ref, bf16[64,96,128]{2,1,0:T(8,128)(2,1)} %get-tuple-element.30.gain_ref, bf16[64,128,128]{2,1,0:T(8,128)(2,1)} %get-tuple-element.27.level_ref, bf16[96,128]{1,0:T(8,128)(2,1)} %constant_dynamic-slice_fusion.3.decoder_ref, ...), custom_call_target="tpu_custom_call" | custom-call | flops 1811939328 | bytes 7864320 | tf_op jit(solution)/shard_map/adjoint/pallas_call | solution.py:308
  470.1 25.7 %adjoint.6.in_ref = bf16[96,64,128]{2,1,0:T(8,128)(2,1)} custom-call(bf16[96,64,128]{2,1,0:T(8,128)(2,1)} %adjoint.5.in_ref, bf16[64,96,128]{2,1,0:T(8,128)(2,1)} %get-tuple-element.29.gain_ref, bf16[64,128,128]{2,1,0:T(8,128)(2,1)} %get-tuple-element.26.level_ref, bf16[96,128]{1,0:T(8,128)(2,1)} %constant_dynamic-slice_fusion.3.decoder_ref, ...), custom_call_target="tpu_custom_call" | custom-call | flops 1811939328 | bytes 7864320 | tf_op jit(solution)/shard_map/adjoint/pallas_call | solution.py:308
  499.3 8.2 %all-to-all-done.7 = bf16[96,64,128]{2,0,1:T(8,128)(2,1)S(1)} async-done(((bf16[96,64,128]{2,0,1:T(8,128)(2,1)}), bf16[96,64,128]{2,0,1:T(8,128)(2,1)S(1)}, u32[]{:S(2)}, u32[]{:S(2)}) %all-to-all-start.7) | async-done | bytes 1572896 | tf_op jit(solution)/shard_map/all_to_all | solution.py:406
  512.0 25.6 %adjoint.7 = bf16[96,64,128]{2,1,0:T(8,128)(2,1)} custom-call(bf16[96,64,128]{2,1,0:T(8,128)(2,1)} %adjoint.6.in_ref, bf16[64,96,128]{2,1,0:T(8,128)(2,1)} %get-tuple-element.28.gain_ref, bf16[64,128,128]{2,1,0:T(8,128)(2,1)} %get-tuple-element.25.level_ref, bf16[96,128]{1,0:T(8,128)(2,1)} %constant_dynamic-slice_fusion.3.decoder_ref, ...), custom_call_target="tpu_custom_call" | custom-call | flops 1811939328 | bytes 7864320 | tf_op jit(solution)/shard_map/adjoint/pallas_call | solution.py:308
  541.3 7.2 %all-to-all-done.6 = bf16[96,64,128]{2,0,1:T(8,128)(2,1)} async-done(((bf16[96,64,128]{2,0,1:T(8,128)(2,1)}), bf16[96,64,128]{2,0,1:T(8,128)(2,1)}, u32[]{:S(2)}, u32[]{:S(2)}) %all-to-all-start.6) | async-done | bytes 1572896 | tf_op jit(solution)/shard_map/all_to_all | solution.py:406
  557.2 32.2 %all-to-all-done.5 = bf16[96,64,128]{2,0,1:T(8,128)(2,1)} async-done(((bf16[96,64,128]{2,0,1:T(8,128)(2,1)}), bf16[96,64,128]{2,0,1:T(8,128)(2,1)}, u32[]{:S(2)}, u32[]{:S(2)}) %all-to-all-start.5) | async-done | bytes 1572896 | tf_op jit(solution)/shard_map/all_to_all | solution.py:406
  592.5 74.3 %all_to_all.91 = bf16[4,768,8,128]{3,2,1,0:T(8,128)(2,1)} all-to-all(bf16[4,768,8,128]{3,2,1,0:T(8,128)(2,1)S(1)} %pad_maximum_fusion.1), channel_id=1, replica_groups=mesh['lead'=4,'space'=8] {'lead'}, dimensions={0} | all-to-all | bytes 12582912 | tf_op jit(solution)/shard_map/all_to_all | solution.py:410
  666.7 9.0 %copy.80 = bf16[1,4,8,128,768]{4,3,2,1,0:T(8,128)(2,1)} copy(bf16[1,4,8,128,768]{3,2,4,1,0:T(8,128)(2,1)} %bitcast.128) | data formatting | bytes 12582912 | tf_op jit(solution)/shard_map/broadcast_in_dim | solution.py:411
  (90 shorter events, 113.2 us)
Async XLA Ops:
  6.5 16.3 %copy-start = (bf16[768,128]{1,0:T(8,128)(2,1)S(1)}, bf16[768,128]{1,0:T(8,128)(2,1)}, u32[]{:S(2)}) copy-start(bf16[768,128]{1,0:T(8,128)(2,1)} %param.22) | copy-start | bytes 589828
  15.6 16.3 %all-to-all-start = ((f32[64,6,128]{2,1,0:T(8,128)}), f32[64,6,128]{2,1,0:T(8,128)S(1)}, u32[]{:S(2)}, u32[]{:S(2)}) async-start(f32[64,6,128]{2,1,0:T(8,128)} %scatter_fusion), calls=%async_computation | async-start | bytes 524288 | tf_op jit(solution)/shard_map/all_to_all | solution.py:448
  82.9 9.1 %copy-start.8 = (s32[128]{0:T(128)S(1)}, s32[128]{0:T(128)}, u32[]{:S(2)}) copy-start(s32[128]{0:T(128)} %constant.216) | copy-start | bytes 1540
  82.9 42.6 %all-to-all-start.1 = ((bf16[8,8,96,128]{3,2,1,0:T(8,128)(2,1)}), bf16[8,8,96,128]{3,2,1,0:T(8,128)(2,1)S(1)}, u32[]{:S(2)}, u32[]{:S(2)}) async-start(bf16[8,8,96,128]{3,2,1,0:T(8,128)(2,1)} %spectrum.4), calls=%async_computation.1 | async-start | bytes 3145728 | tf_op jit(solution)/shard_map/all_to_all | solution.py:371
  147.5 3.8 copy-start.7
  147.5 41.0 %all-to-all-start.2 = ((bf16[8,8,96,128]{3,2,1,0:T(8,128)(2,1)}), bf16[8,8,96,128]{3,2,1,0:T(8,128)(2,1)S(1)}, u32[]{:S(2)}, u32[]{:S(2)}) async-start(bf16[8,8,96,128]{3,2,1,0:T(8,128)(2,1)} %spectrum.5), calls=%async_computation.2 | async-start | bytes 3145728 | tf_op jit(solution)/shard_map/all_to_all | solution.py:371
  151.3 240.6 %all-gather.3.cloned.1.call-start = ((), (), s32[]{:S(2)}) async-start(), calls=%async_computation.10 | async-start | bytes 2359296 | tf_op jit(solution)/shard_map/all_gather | solution.py:384
  152.3 7.7 %collective-permute-start.5 = (bf16[8,128,128]{2,1,0:T(8,128)(2,1)}, bf16[8,128,128]{2,1,0:T(8,128)(2,1)S(1)}, u32[]{:S(2)}, u32[]{:S(2)}) collective-permute-start(bf16[8,128,128]{2,1,0:T(8,128)(2,1)} %get-tuple-element.37), channel_id=1, source_target_pairs={{0,24},{8,0},{16,8},{24,16},{1,25},{9,1},{17,9},{25,17},{2,26},{10... | collective-permute-start | bytes 786440 | tf_op jit(solution)/shard_map/ppermute | solution.py:353
  153.1 13.6 %collective-permute-start.4 = (bf16[8,128,128]{2,1,0:T(8,128)(2,1)}, bf16[8,128,128]{2,1,0:T(8,128)(2,1)S(1)}, u32[]{:S(2)}, u32[]{:S(2)}) collective-permute-start(bf16[8,128,128]{2,1,0:T(8,128)(2,1)} %get-tuple-element.38), channel_id=1, source_target_pairs={{0,16},{8,24},{16,0},{24,8},{1,17},{9,25},{17,1},{25,9},{2,18},{10... | collective-permute-start | bytes 786440 | tf_op jit(solution)/shard_map/ppermute | solution.py:353
  153.8 13.0 %collective-permute-start.3 = (bf16[8,128,128]{2,1,0:T(8,128)(2,1)S(1)}, bf16[8,128,128]{2,1,0:T(8,128)(2,1)S(1)}, u32[]{:S(2)}, u32[]{:S(2)}) collective-permute-start(bf16[8,128,128]{2,1,0:T(8,128)(2,1)S(1)} %get-tuple-element.39), channel_id=1, source_target_pairs={{0,8},{8,16},{16,24},{24,0},{1,9},{9,17},{17,25},{25,1},{2,10},{10... | collective-permute-start | bytes 786440 | tf_op jit(solution)/shard_map/ppermute | solution.py:353
  188.5 7.5 %copy-start.3 = (bf16[8,8,96,128]{3,2,1,0:T(8,128)(2,1)}, bf16[8,8,96,128]{3,2,1,0:T(8,128)(2,1)S(1)}, u32[]{:S(2)}) copy-start(bf16[8,8,96,128]{3,2,1,0:T(8,128)(2,1)S(1)} %all-to-all-done.2) | copy-start | bytes 4718596
  188.5 239.1 %all-gather.5.cloned.1.call-start = ((), (), s32[]{:S(2)}) async-start(), calls=%async_computation.11 | async-start | bytes 7077888 | tf_op jit(solution)/shard_map/all_gather | solution.py:385
  280.0 4.6 copy-start.5
  280.0 6.1 copy-start.2
  280.0 72.3 %all-to-all-start.4 = ((bf16[8,8,96,128]{3,2,1,0:T(8,128)(2,1)}), bf16[8,8,96,128]{3,2,1,0:T(8,128)(2,1)}, u32[]{:S(2)}, u32[]{:S(2)}) async-start(bf16[8,8,96,128]{3,2,1,0:T(8,128)(2,1)} %spectrum.7), calls=%async_computation.4 | async-start | bytes 3145728 | tf_op jit(solution)/shard_map/all_to_all | solution.py:371
  284.6 99.3 %collective-permute-start.1 = (bf16[64,96,128]{2,1,0:T(8,128)(2,1)S(1)}, bf16[64,96,128]{2,1,0:T(8,128)(2,1)}, u32[]{:S(2)}, u32[]{:S(2)}) collective-permute-start(bf16[64,96,128]{2,1,0:T(8,128)(2,1)S(1)} %copy-done.5), channel_id=1, source_target_pairs={{0,16},{8,24},{16,0},{24,8},{1,17},{9,25},{17,1},{25,9},{2,18},{10... | collective-permute-start | bytes 4718600 | tf_op jit(solution)/shard_map/ppermute | solution.py:353
  286.2 97.7 %collective-permute-start = (bf16[64,96,128]{2,1,0:T(8,128)(2,1)S(1)}, bf16[64,96,128]{2,1,0:T(8,128)(2,1)}, u32[]{:S(2)}, u32[]{:S(2)}) collective-permute-start(bf16[64,96,128]{2,1,0:T(8,128)(2,1)S(1)} %copy-done.2), channel_id=1, source_target_pairs={{0,8},{8,16},{16,24},{24,0},{1,9},{9,17},{17,25},{25,1},{2,10},{10... | collective-permute-start | bytes 4718600 | tf_op jit(solution)/shard_map/ppermute | solution.py:353
  367.0 18.4 %collective-permute-start.2 = (bf16[64,96,128]{2,1,0:T(8,128)(2,1)}, bf16[64,96,128]{2,1,0:T(8,128)(2,1)S(1)}, u32[]{:S(2)}, u32[]{:S(2)}) collective-permute-start(bf16[64,96,128]{2,1,0:T(8,128)(2,1)} %slopes.7), channel_id=1, source_target_pairs={{0,24},{8,0},{16,8},{24,16},{1,25},{9,1},{17,9},{25,17},{2,26},{10... | collective-permute-start | bytes 4718600 | tf_op jit(solution)/shard_map/ppermute | solution.py:353
  422.6 43.9 %all-to-all-start.8 = ((bf16[96,64,128]{2,0,1:T(8,128)(2,1)}), bf16[96,64,128]{2,0,1:T(8,128)(2,1)S(1)}, u32[]{:S(2)}, u32[]{:S(2)}) async-start(bf16[96,64,128]{2,0,1:T(8,128)(2,1)} %copy.77), calls=%async_computation.8 | async-start | bytes 3145728 | tf_op jit(solution)/shard_map/all_to_all | solution.py:406
  466.5 41.0 %all-to-all-start.7 = ((bf16[96,64,128]{2,0,1:T(8,128)(2,1)}), bf16[96,64,128]{2,0,1:T(8,128)(2,1)S(1)}, u32[]{:S(2)}, u32[]{:S(2)}) async-start(bf16[96,64,128]{2,0,1:T(8,128)(2,1)} %copy.74), calls=%async_computation.7 | async-start | bytes 3145728 | tf_op jit(solution)/shard_map/all_to_all | solution.py:406
  507.5 41.0 %all-to-all-start.6 = ((bf16[96,64,128]{2,0,1:T(8,128)(2,1)}), bf16[96,64,128]{2,0,1:T(8,128)(2,1)}, u32[]{:S(2)}, u32[]{:S(2)}) async-start(bf16[96,64,128]{2,0,1:T(8,128)(2,1)} %copy.71), calls=%async_computation.6 | async-start | bytes 3145728 | tf_op jit(solution)/shard_map/all_to_all | solution.py:406
  548.5 40.9 %all-to-all-start.5 = ((bf16[96,64,128]{2,0,1:T(8,128)(2,1)}), bf16[96,64,128]{2,0,1:T(8,128)(2,1)}, u32[]{:S(2)}, u32[]{:S(2)}) async-start(bf16[96,64,128]{2,0,1:T(8,128)(2,1)} %copy.68), calls=%async_computation.5 | async-start | bytes 3145728 | tf_op jit(solution)/shard_map/all_to_all | solution.py:406
  589.5 2.1 copy-start.6
  666.7 9.0 %copy-start.1 = (bf16[768,128]{1,0:T(8,128)(2,1)S(1)}, bf16[768,128]{1,0:T(8,128)(2,1)}, u32[]{:S(2)}) copy-start(bf16[768,128]{1,0:T(8,128)(2,1)} %param.22) | copy-start | bytes 589828
  (1 other events, 1.1 us)
Sparse Core Ops, SparseCore 0:
  188.6 69.0 all-gather.2
  259.9 120.8 all-gather.4
